TPU v7x, 32 devices: a whole 2x2x4 slice. The times are simulated.
32 devices in a mesh: rows: 8 (over z, y), pair: 4 (over x, core).
Axes of the slice: x: 2, y: 2, z: 4, core: 2. Of those that a mesh axis runs over, the one named last changes fastest.
Arguments:
- a_tiles: bfloat16 [2048, 8, 4096], P(('rows', 'pair')), may hold values from -2.09375 to 2.09375
- p_tiles: bfloat16 [2048, 4096], P(('rows', 'pair')), may hold values from -0.75 to 0.75
- a_cols: int32 [2048, 8], P(('rows', 'pair')), may hold values from 0 to 2047, as said below
- tile_group: int32 [2048, 8], P(('rows', 'pair')), may hold values from 0 to 1
- coarse_slots: int32 [2048, 2], P(('rows', 'pair')), may hold values from 0 to 15
- aggregate: int32 [2048], P(('rows', 'pair')), may hold values from 0 to 127, as said below
Outputs:
- coarse_tiles: float32 [128, 16, 4096], P(('rows', 'pair'))
Inputs may be any that keep to these rules, and one draw needn't show every extreme that they name: `a_cols`: each operator tile's column block lies within 2 block rows of its own block row. `aggregate`: coarse block rows come in groups of 16 consecutive ones, group g held by index g of rows; the fine block rows of one device name at most 16 rows of one group, and one group, drawn from the seed, gets exactly 16 from every device.
All inputs are finite; a program needn't handle non-finite values.
Results may differ from a plain program's by a relative error of at most 0.0041.
Values may be sent and summed in bfloat16 or wider, within the bound.
A program may use at most 128 MiB of HBM per device.

v0:
```python
import functools

import jax
import jax.numpy as jnp
from jax import lax
from jax.experimental import pallas as pl
from jax.experimental.pallas import tpu as pltpu
from jax.sharding import PartitionSpec as P

BLK = 64
KA = 8
KS = 2
KC = 16
HB = 2
RATIO = 16
LANES = 128
NEAR = 2 * HB + 1
CHUNK = 8
STEPS = 8
BOTH = ("rows", "pair")


def extended(array, width):
    devices, length = lax.axis_size(BOTH), array.shape[0]
    up = [(i, i + 1) for i in range(devices - 1)]
    down = [(j, i) for i, j in up]
    before = lax.ppermute(array[length - width :], BOTH, up)
    after = lax.ppermute(array[:width], BOTH, down)
    return jnp.concatenate([before, array, after], axis=0)


def iota(shape, dim):
    return lax.broadcasted_iota(jnp.int32, shape, dim)


def put_diagonal(flat, want, low):
    flat = flat.astype(jnp.float32)
    turned = pltpu.roll(flat, BLK, 1)
    zero = jnp.zeros_like(flat)
    parts = jnp.concatenate(
        [
            jnp.where(low, flat, zero),
            jnp.where(low, turned, zero),
            jnp.where(low, zero, turned),
            jnp.where(low, zero, flat),
        ],
        axis=0,
    ).astype(jnp.bfloat16)
    return jnp.dot(want, parts, preferred_element_type=jnp.float32).astype(jnp.bfloat16)


def constants():
    q = BLK // 2
    r, k = iota((LANES, LANES), 0), iota((LANES, LANES), 1)
    want = jnp.where(
        (r // BLK == k // BLK) & (r % BLK == 2 * (k % q) + (k // q) % 2), 1.0, 0.0
    ).astype(jnp.bfloat16)
    eye = jnp.where(r == k, 1.0, 0.0).astype(jnp.bfloat16)
    spread = jnp.where(
        iota((q, q * KA), 0) == iota((q, q * KA), 1) // KA, 1.0, 0.0
    ).astype(jnp.bfloat16)
    low = iota((q, LANES), 1) < BLK
    return want, eye, spread, low


def row_terms(read, code, group, near, own, eye, spread, low):
    q = BLK // 2
    tiles = jnp.concatenate([read(c).astype(jnp.float32) for c in range(q)], axis=0)
    tiles = tiles.astype(jnp.bfloat16)

    def picked(j):
        one = jnp.where(code == j, 1.0, 0.0)
        pair = jnp.concatenate([one, one], axis=0).astype(jnp.bfloat16)
        return jnp.broadcast_to(pair[None], (q // 2,) + pair.shape).reshape(tiles.shape)

    left = jnp.concatenate([tiles * picked(j) for j in range(NEAR)], axis=1)
    products = jnp.dot(left, near, preferred_element_type=jnp.float32).astype(jnp.bfloat16)
    turned = lax.dot_general(
        eye, own, (((1,), (1,)), ((), ())), preferred_element_type=jnp.float32
    ).astype(jnp.bfloat16)
    wide = jnp.dot(turned, spread, preferred_element_type=jnp.float32).astype(jnp.bfloat16)
    rows = jnp.concatenate(
        [wide * jnp.where(group == s, 1.0, 0.0).astype(jnp.bfloat16) for s in range(KS)], axis=0
    )
    full = jnp.dot(rows, products, preferred_element_type=jnp.float32)
    terms = []
    for s in range(KS):
        part = full[s * LANES : (s + 1) * LANES]
        terms.append(
            jnp.where(low, part[:q], part[3 * q :])
            + pltpu.roll(jnp.where(low, part[q : 2 * q], part[2 * q : 3 * q]), BLK, 1)
        )
    return terms


def terms_kernel(a_ref, p_ref, code_ref, group_ref, out_ref, diag, stage):
    step = pl.program_id(0)
    q = BLK // 2
    want, eye, spread, low = constants()

    @pl.when(step == 0)
    def _():
        def one(t, _):
            diag[pl.ds(pl.multiple_of(t * LANES, LANES), LANES), :] = put_diagonal(p_ref[t], want, low)
            return 0

        lax.fori_loop(0, p_ref.shape[0], one, 0, unroll=4)

    for i in range(CHUNK):
        row = step * CHUNK + i
        terms = row_terms(
            lambda c: a_ref[i, :, c * LANES : (c + 1) * LANES],
            code_ref[i],
            group_ref[i],
            diag[pl.ds(pl.multiple_of(row * LANES, LANES), NEAR * LANES), :],
            p_ref[row + HB],
            eye,
            spread,
            low,
        )
        for s in range(KS):
            stage[pl.ds(s * CHUNK + i, q, stride=KS * CHUNK), :] = terms[s]
    out_ref[...] = stage[...].astype(jnp.bfloat16).reshape(out_ref.shape)


def row_codes(a_cols, tile_group):
    fine_rows = a_cols.shape[0]
    q = BLK // 2
    own = lax.axis_index(BOTH) * fine_rows + jnp.arange(fine_rows, dtype=jnp.int32)
    offset = a_cols - own[:, None] + HB
    code = jnp.broadcast_to(offset[:, :, None], (fine_rows, KA, LANES))
    group = jnp.tile(tile_group, (1, q)).reshape(fine_rows, 1, q * KA)
    return code, group


def local_terms(a_tiles, p_tiles, a_cols, tile_group):
    fine_rows = a_tiles.shape[0]
    q = BLK // 2
    near_p = extended(p_tiles, HB).reshape(fine_rows + 2 * HB, q, LANES)
    code, group = row_codes(a_cols, tile_group)
    steps = fine_rows // CHUNK
    return pl.pallas_call(
        terms_kernel,
        grid=(steps,),
        in_specs=[
            pl.BlockSpec((CHUNK, KA, BLK * BLK), lambda g: (g, 0, 0)),
            pl.BlockSpec((fine_rows + 2 * HB, q, LANES), lambda g: (0, 0, 0)),
            pl.BlockSpec((CHUNK, KA, LANES), lambda g: (g, 0, 0)),
            pl.BlockSpec((CHUNK, 1, q * KA), lambda g: (g, 0, 0)),
        ],
        out_specs=pl.BlockSpec((q, KS * CHUNK, LANES), lambda g: (0, g, 0)),
        out_shape=jax.ShapeDtypeStruct((q, fine_rows * KS, LANES), jnp.bfloat16),
        scratch_shapes=[
            pltpu.VMEM(((fine_rows + 2 * HB) * LANES, LANES), jnp.bfloat16),
            pltpu.VMEM((q * KS * CHUNK, LANES), jnp.float32),
        ],
        compiler_params=pltpu.CompilerParams(vmem_limit_bytes=40 * 1024 * 1024),
    )(a_tiles, near_p, code, group)


def in_term_order(values):
    rows = values.shape[0]
    return values.reshape(rows // CHUNK, CHUNK, KS).transpose(0, 2, 1).reshape(rows * KS)


def exchange_kernel(rows_count, pair_count, a_hbm, p_ref, code_ref, group_ref, target_ref, out_ref, a_ref, diag, stage, halo, term_ref, got, goals, sums, parts, a_came, halo_sent, halo_came, sent, came, goal_sent, goal_came, sum_sent, sum_came):
    my_row, my_pair = lax.axis_index("rows"), lax.axis_index("pair")
    devices = rows_count * pair_count
    me = my_row * pair_count + my_pair
    tiles = parts.shape[1]
    block = pair_count * tiles

    def at(device):
        return (lax.div(device, pair_count), lax.rem(device, pair_count))

    def copy(src, dst, send_sem, recv_sem, device):
        return pltpu.make_async_remote_copy(
            src_ref=src,
            dst_ref=dst,
            send_sem=send_sem,
            recv_sem=recv_sem,
            device_id=at(device),
            device_id_type=pl.DeviceIdType.MESH,
        )

    fine_rows = p_ref.shape[0]
    q = BLK // 2
    steps = STEPS
    span = fine_rows // steps
    terms_span = span * KS
    ahead, behind = lax.rem(me + 1, devices), lax.rem(me + devices - 1, devices)

    def a_copy(step):
        rows = pl.ds(pl.multiple_of(lax.rem(step + 1, steps) * span, span), span)
        return pltpu.make_async_copy(a_hbm.at[rows], a_ref.at[rows], a_came.at[step])

    def term_copy(device, slot):
        return copy(term_ref.at[device], got.at[slot], sent.at[device], came.at[slot], device)

    def term_part(device, slot, part):
        rows = pl.ds(pl.multiple_of(part * terms_span, terms_span), terms_span)
        return copy(term_ref.at[device, rows], got.at[slot, rows], sent.at[device], came.at[slot], device)

    halo_up = copy(p_ref.at[pl.ds(fine_rows - HB, HB)], halo.at[pl.ds(0, HB)], halo_sent.at[0], halo_came.at[0], ahead)
    halo_down = copy(p_ref.at[pl.ds(0, HB)], halo.at[pl.ds(HB, HB)], halo_sent.at[1], halo_came.at[1], behind)

    def goal_copy(device, slot):
        return copy(target_ref, goals.at[slot], goal_sent.at[device], goal_came.at[slot], device)

    def sum_copy(device, slot):
        rows = pl.ds(pl.multiple_of(device * tiles, tiles), tiles)
        return copy(sums.at[rows], parts.at[slot], sum_sent.at[device], sum_came.at[slot], device)

    barrier = pltpu.get_barrier_semaphore()
    offsets = sorted(range(1, devices), key=lambda o: abs(o - devices // 2))
    for o in offsets:
        pl.semaphore_signal(
            barrier, inc=1, device_id=at(lax.rem(me + o, devices)), device_id_type=pl.DeviceIdType.MESH
        )
    for step in range(steps):
        a_copy(step).start()
    want, eye, spread, low = constants()

    def own_diagonal(t, _):
        diag[pl.ds(pl.multiple_of((t + HB) * LANES, LANES), LANES), :] = put_diagonal(p_ref[t], want, low)
        return 0

    lax.fori_loop(0, fine_rows, own_diagonal, 0, unroll=4)
    pl.semaphore_wait(barrier, devices - 1)
    halo_up.start()
    halo_down.start()
    for o in offsets:
        other = lax.rem(me + o, devices)
        goal_copy(other, me).start()
    goals[me] = target_ref[...]

    def quarter(step, _):
        part = lax.rem(step + 1, steps)
        a_copy(step).wait()

        @pl.when(step == steps - 2)
        def _():
            halo_up.wait_recv()
            halo_down.wait_recv()
            for t in range(HB):
                diag[t * LANES : (t + 1) * LANES, :] = put_diagonal(halo[t], want, low)
                last = fine_rows + HB + t
                diag[last * LANES : (last + 1) * LANES, :] = put_diagonal(halo[HB + t], want, low)

        def chunk(c, _):
            at_chunk = part * (span // CHUNK) + c

            for i in range(CHUNK):
                row = at_chunk * CHUNK + i
                terms = row_terms(
                    lambda col: a_ref[row, :, col * LANES : (col + 1) * LANES],
                    code_ref[row],
                    group_ref[row],
                    diag[pl.ds(pl.multiple_of(row * LANES, LANES), NEAR * LANES), :],
                    p_ref[row],
                    eye,
                    spread,
                    low,
                )
                for s in range(KS):
                    stage[pl.ds(s * CHUNK + i, q, stride=KS * CHUNK), :] = terms[s]
            rows = pl.ds(pl.multiple_of(at_chunk * KS * CHUNK, KS * CHUNK), KS * CHUNK)
            term_ref[:, rows, :] = stage[...].astype(jnp.bfloat16).reshape(q, KS * CHUNK, LANES)
            return 0

        lax.fori_loop(0, span // CHUNK, chunk, 0)
        for o in offsets:
            term_part(lax.rem(me + o, devices), me, part).start()
        return 0

    lax.fori_loop(0, steps, quarter, 0)
    got[me] = term_ref[me]
    for o in offsets[::-1]:
        other = lax.rem(me + o, devices)
        goal_copy(other, other).wait_recv()
        term_copy(other, other).wait_recv()

    goal = jnp.concatenate([goals[j] for j in range(devices)], axis=1)
    for k in sorted(range(rows_count), key=lambda o: abs(o - rows_count // 2)):
        row = lax.rem(my_row + k, rows_count)
        first = row * block
        hot = jnp.where(first + iota((block, goal.shape[1]), 0) == goal, 1.0, 0.0).astype(jnp.bfloat16)
        sums[pl.ds(pl.multiple_of(first, block), block), :] = jnp.dot(
            hot, got[...].reshape(-1, LANES), preferred_element_type=jnp.float32
        ).astype(jnp.bfloat16)
        for o in range(0 if k else 1, pair_count):
            other = row * pair_count + lax.rem(my_pair + o, pair_count)
            sum_copy(other, me).start()
    parts[me] = sums[pl.ds(pl.multiple_of(me * tiles, tiles), tiles), :]
    for o in offsets:
        other = lax.rem(me + o, devices)
        sum_copy(other, other).wait_recv()

    low = iota((tiles, LANES), 1) < BLK
    half = devices * BLK
    for m in range(devices // 2):
        one, two = parts[2 * m].astype(jnp.float32), parts[2 * m + 1].astype(jnp.float32)
        to = m * LANES
        out_ref[:, to : to + LANES] = jnp.where(low, one, pltpu.roll(two, BLK, 1))
        out_ref[:, half + to : half + to + LANES] = jnp.where(low, pltpu.roll(one, BLK, 1), two)
    halo_up.wait_send()
    halo_down.wait_send()
    for o in offsets:
        other = lax.rem(me + o, devices)
        term_copy(other, me).wait_send()
        goal_copy(other, me).wait_send()
        sum_copy(other, me).wait_send()


def exchanged(a_tiles, p_tiles, a_cols, tile_group, targets, tiles):
    fine_rows = a_tiles.shape[0]
    count, q = fine_rows * KS, BLK // 2
    rows_count, pair_count = lax.axis_size("rows"), lax.axis_size("pair")
    devices = rows_count * pair_count
    code, group = row_codes(a_cols, tile_group)
    whole = pl.BlockSpec(memory_space=pltpu.VMEM)
    return pl.pallas_call(
        functools.partial(exchange_kernel, rows_count, pair_count),
        in_specs=[pl.BlockSpec(memory_space=pltpu.HBM)] + [whole] * 4,
        out_specs=whole,
        out_shape=jax.ShapeDtypeStruct((tiles, devices * LANES), jnp.float32),
        scratch_shapes=[
            pltpu.VMEM(a_tiles.shape, jnp.bfloat16),
            pltpu.VMEM(((fine_rows + 2 * HB) * LANES, LANES), jnp.bfloat16),
            pltpu.VMEM((q * KS * CHUNK, LANES), jnp.float32),
            pltpu.VMEM((2 * HB, q, LANES), jnp.bfloat16),
            pltpu.VMEM((devices, count, LANES), jnp.bfloat16),
            pltpu.VMEM((devices, count, LANES), jnp.bfloat16),
            pltpu.VMEM((devices, 1, count), jnp.int32),
            pltpu.VMEM((devices * tiles, LANES), jnp.bfloat16),
            pltpu.VMEM((devices, tiles, LANES), jnp.bfloat16),
            pltpu.SemaphoreType.DMA((STEPS,)),
            pltpu.SemaphoreType.DMA((2,)),
            pltpu.SemaphoreType.DMA((2,)),
        ]
        + [pltpu.SemaphoreType.DMA((devices,))] * 6,
        compiler_params=pltpu.CompilerParams(
            collective_id=0, has_side_effects=True, vmem_limit_bytes=48 * 1024 * 1024
        ),
    )(a_tiles, p_tiles.reshape(fine_rows, q, LANES), code, group, targets)


def routed(terms, coarse_slots, aggregate):
    fine_rows = aggregate.shape[0]
    q = BLK // 2
    width = BLK * BLK
    rows_count, pair_count = lax.axis_size("rows"), lax.axis_size("pair")
    flat = terms.reshape(q, fine_rows // CHUNK, KS, CHUNK, 2, BLK)
    flat = flat.transpose(1, 3, 2, 4, 0, 5).reshape(fine_rows, KS, width)
    group_size = fine_rows // RATIO * pair_count
    capacity = 2 * fine_rows // rows_count
    dest_group = aggregate // group_size
    local_rows = aggregate - dest_group * group_size
    targets = local_rows[:, None] * KC + coarse_slots
    order = jnp.arange(fine_rows)
    same = (dest_group[:, None] == dest_group[None, :]) & (order[None, :] < order[:, None])
    position = dest_group * capacity + jnp.sum(same.astype(jnp.int32), axis=1)

    def exchange(values):
        buffer = jnp.zeros((rows_count * capacity,) + values.shape[1:], values.dtype)
        buffer = buffer.at[position].set(values)
        return lax.all_to_all(buffer, "rows", split_axis=0, concat_axis=0, tiled=True)

    got = exchange(flat).reshape(-1, width).astype(jnp.float32)
    panel = jax.ops.segment_sum(
        got, exchange(targets).reshape(-1), num_segments=group_size * KC
    )
    panel = panel.reshape(group_size, KC, width)
    return lax.psum_scatter(panel, "pair", scatter_dimension=0, tiled=True)


def body(a_tiles, p_tiles, a_cols, tile_group, coarse_slots, aggregate):
    fine_rows, width = p_tiles.shape
    devices = lax.axis_size(BOTH)
    if devices * LANES != width:
        return routed(local_terms(a_tiles, p_tiles, a_cols, tile_group), coarse_slots, aggregate)
    targets = in_term_order(aggregate[:, None] * KC + coarse_slots).reshape(1, -1)
    tiles = fine_rows // RATIO * KC
    result = exchanged(a_tiles, p_tiles, a_cols, tile_group, targets, tiles)
    return result.reshape(fine_rows // RATIO, KC, width)


def solution(mesh):
    return jax.shard_map(
        body,
        mesh=mesh,
        in_specs=(
            P(BOTH, None, None),
            P(BOTH, None),
            P(BOTH, None),
            P(BOTH, None),
            P(BOTH, None),
            P(BOTH),
        ),
        out_specs=P(BOTH, None, None),
        check_vma=False,
    )
```

profile of v0, /device:TPU:0, one launch (start us, length us, event | category | flops | bytes accessed | tf_op | source)
XLA Modules:
  0.0 56.7 jit_solution(3270370383290941949)
XLA Ops:
  0.0 0.0 copy-start
  0.0 0.7 %broadcast_multiply_fusion = s32[64]{0:T(128)S(1)} fusion(s32[64]{0:T(128)} %param.11), kind=kLoop, calls=%fused_computation.4 | loop fusion | flops 64 | bytes 512 | tf_op jit(solution)/shard_map/mul | solution.py:382
  0.7 0.7 %broadcast_add_fusion = s32[64,2]{0,1:T(2,128)S(1)} fusion(s32[64,2]{0,1:T(2,128)} %param.10, s32[64]{0:T(128)S(1)} %broadcast_multiply_fusion), kind=kLoop, calls=%fused_computation.2 | loop fusion | flops 128 | bytes 1280 | tf_op jit(solution)/shard_map/add | solution.py:382
  1.4 0.7 %subtract_add_fusion = s32[64,8]{0,1:T(8,128)S(1)} fusion(s32[64,8]{0,1:T(8,128)} %param.8, s32[64]{0:T(128)S(1)} %iota_add_fusion), kind=kLoop, calls=%fused_computation.1 | loop fusion | flops 1024 | bytes 4352 | tf_op jit(solution)/shard_map/add | solution.py:130
  2.0 0.1 reshape.23
  2.1 0.1 reshape_reshape.3.target_ref
  2.2 0.1 copy.10
  2.3 0.0 copy-done
  2.3 0.1 copy.12.group_ref
  2.4 0.1 broadcast_in_dim.2.code_ref
  2.6 1.1 %copy.13 = bf16[8,8,32,128]{3,2,1,0:T(8,128)(2,1)S(1)} copy(bf16[8,8,32,128]{3,1,2,0:T(8,128)(2,1)} %bitcast.10) | data formatting | bytes 1048576
  3.7 0.0 copy-start.1
  3.7 2.2 %copy-done.1 = bf16[64,8,4096]{2,1,0:T(8,128)(2,1)S(1)} copy-done((bf16[64,8,4096]{2,1,0:T(8,128)(2,1)S(1)}, bf16[64,8,4096]{2,1,0:T(8,128)(2,1)}, u32[]{:S(2)}) %copy-start.1) | copy-done | bytes 4194328
  5.9 49.8 %shard_map.64 = f32[64,4096]{1,0:T(8,128)S(1)} custom-call(bf16[64,8,4096]{2,1,0:T(8,128)(2,1)S(1)} %copy-done.1, bf16[64,32,128]{2,1,0:T(8,128)(2,1)S(1)} %bitcast.9, s32[64,8,128]{2,1,0:T(8,128)S(1)} %broadcast_in_dim.2.code_ref, s32[64,1,256]{2,1,0:T(1,128)S(1)} %copy.12.group_ref, s32[1,128]{1,0:T(1,128)S(1)} %reshape_reshape.3.target_ref), custom_call_target="tpu_custom_call" | custom-call | tf_op jit(solution)/shard_map/pallas_call | solution.py:322
  55.7 1.0 %copy.15 = f32[4,16,4096]{2,1,0:T(8,128)} copy(f32[4,16,4096]{2,1,0:T(8,128)S(1)} %bitcast.8) | data formatting | bytes 2097152
  (3 shorter events, 0.0 us)
Async XLA Ops:
  0.0 2.3 %copy-start = (s32[64,8]{0,1:T(8,128)S(1)}, s32[64,8]{0,1:T(8,128)}, u32[]{:S(2)}) copy-start(s32[64,8]{0,1:T(8,128)} %param.9) | copy-start | bytes 6148
  3.7 2.2 %copy-start.1 = (bf16[64,8,4096]{2,1,0:T(8,128)(2,1)S(1)}, bf16[64,8,4096]{2,1,0:T(8,128)(2,1)}, u32[]{:S(2)}) copy-start(bf16[64,8,4096]{2,1,0:T(8,128)(2,1)} %a_hbm.1) | copy-start | bytes 12582916
where the time goes:
time: 57 us; the launch traced here: 56.7 us
  Pallas kernels  49.8 us (87%)
  local copies, waits for them, and re-layouts  4.79 us (8%)
  other arithmetic  2.04 us (4%)
    pallas_call x1, Pallas kernels, exchanged(): pl.pallas_call(functools.partial(exchange_kernel, rows_count, pair_count)...  49.8 us
    unnamed x6, local copies, waits for them, and re-layouts  4.3 us

commit v1 on v0

v1 whole, which is shorter than its diff:
```python
import functools

import jax
import jax.numpy as jnp
from jax import lax
from jax.experimental import pallas as pl
from jax.experimental.pallas import tpu as pltpu
from jax.sharding import PartitionSpec as P

BLK = 64
KA = 8
KS = 2
KC = 16
HB = 2
RATIO = 16
LANES = 128
NEAR = 2 * HB + 1
CHUNK = 8
BOTH = ("rows", "pair")


def extended(array, width):
    devices, length = lax.axis_size(BOTH), array.shape[0]
    up = [(i, i + 1) for i in range(devices - 1)]
    down = [(j, i) for i, j in up]
    before = lax.ppermute(array[length - width :], BOTH, up)
    after = lax.ppermute(array[:width], BOTH, down)
    return jnp.concatenate([before, array, after], axis=0)


def iota(shape, dim):
    return lax.broadcasted_iota(jnp.int32, shape, dim)


def put_diagonal(flat, want, low):
    flat = flat.astype(jnp.float32)
    turned = pltpu.roll(flat, BLK, 1)
    zero = jnp.zeros_like(flat)
    parts = jnp.concatenate(
        [
            jnp.where(low, flat, zero),
            jnp.where(low, turned, zero),
            jnp.where(low, zero, turned),
            jnp.where(low, zero, flat),
        ],
        axis=0,
    ).astype(jnp.bfloat16)
    return jnp.dot(want, parts, preferred_element_type=jnp.float32).astype(jnp.bfloat16)


def constants():
    q = BLK // 2
    r, k = iota((LANES, LANES), 0), iota((LANES, LANES), 1)
    want = jnp.where(
        (r // BLK == k // BLK) & (r % BLK == 2 * (k % q) + (k // q) % 2), 1.0, 0.0
    ).astype(jnp.bfloat16)
    eye = jnp.where(r == k, 1.0, 0.0).astype(jnp.bfloat16)
    spread = jnp.where(
        iota((q, q * KA), 0) == iota((q, q * KA), 1) // KA, 1.0, 0.0
    ).astype(jnp.bfloat16)
    low = iota((q, LANES), 1) < BLK
    return want, eye, spread, low


def row_terms(read, code, group, near, own, eye, spread, low):
    q = BLK // 2
    tiles = jnp.concatenate([read(c).astype(jnp.float32) for c in range(q)], axis=0)
    tiles = tiles.astype(jnp.bfloat16)

    def picked(j):
        one = jnp.where(code == j, 1.0, 0.0)
        pair = jnp.concatenate([one, one], axis=0).astype(jnp.bfloat16)
        return jnp.broadcast_to(pair[None], (q // 2,) + pair.shape).reshape(tiles.shape)

    left = jnp.concatenate([tiles * picked(j) for j in range(NEAR)], axis=1)
    products = jnp.dot(left, near, preferred_element_type=jnp.float32).astype(jnp.bfloat16)
    turned = lax.dot_general(
        eye, own, (((1,), (1,)), ((), ())), preferred_element_type=jnp.float32
    ).astype(jnp.bfloat16)
    wide = jnp.dot(turned, spread, preferred_element_type=jnp.float32).astype(jnp.bfloat16)
    rows = jnp.concatenate(
        [wide * jnp.where(group == s, 1.0, 0.0).astype(jnp.bfloat16) for s in range(KS)], axis=0
    )
    full = jnp.dot(rows, products, preferred_element_type=jnp.float32)
    terms = []
    for s in range(KS):
        part = full[s * LANES : (s + 1) * LANES]
        terms.append(
            jnp.where(low, part[:q], part[3 * q :])
            + pltpu.roll(jnp.where(low, part[q : 2 * q], part[2 * q : 3 * q]), BLK, 1)
        )
    return terms


def terms_kernel(a_ref, p_ref, code_ref, group_ref, out_ref, diag, stage):
    step = pl.program_id(0)
    q = BLK // 2
    want, eye, spread, low = constants()

    @pl.when(step == 0)
    def _():
        def one(t, _):
            diag[pl.ds(pl.multiple_of(t * LANES, LANES), LANES), :] = put_diagonal(p_ref[t], want, low)
            return 0

        lax.fori_loop(0, p_ref.shape[0], one, 0, unroll=4)

    for i in range(CHUNK):
        row = step * CHUNK + i
        terms = row_terms(
            lambda c: a_ref[i, :, c * LANES : (c + 1) * LANES],
            code_ref[i],
            group_ref[i],
            diag[pl.ds(pl.multiple_of(row * LANES, LANES), NEAR * LANES), :],
            p_ref[row + HB],
            eye,
            spread,
            low,
        )
        for s in range(KS):
            stage[pl.ds(s * CHUNK + i, q, stride=KS * CHUNK), :] = terms[s]
    out_ref[...] = stage[...].astype(jnp.bfloat16).reshape(out_ref.shape)


def row_codes(a_cols, tile_group):
    fine_rows = a_cols.shape[0]
    q = BLK // 2
    own = lax.axis_index(BOTH) * fine_rows + jnp.arange(fine_rows, dtype=jnp.int32)
    offset = a_cols - own[:, None] + HB
    code = jnp.broadcast_to(offset[:, :, None], (fine_rows, KA, LANES))
    group = jnp.tile(tile_group, (1, q)).reshape(fine_rows, 1, q * KA)
    return code, group


def local_terms(a_tiles, p_tiles, a_cols, tile_group):
    fine_rows = a_tiles.shape[0]
    q = BLK // 2
    near_p = extended(p_tiles, HB).reshape(fine_rows + 2 * HB, q, LANES)
    code, group = row_codes(a_cols, tile_group)
    steps = fine_rows // CHUNK
    return pl.pallas_call(
        terms_kernel,
        grid=(steps,),
        in_specs=[
            pl.BlockSpec((CHUNK, KA, BLK * BLK), lambda g: (g, 0, 0)),
            pl.BlockSpec((fine_rows + 2 * HB, q, LANES), lambda g: (0, 0, 0)),
            pl.BlockSpec((CHUNK, KA, LANES), lambda g: (g, 0, 0)),
            pl.BlockSpec((CHUNK, 1, q * KA), lambda g: (g, 0, 0)),
        ],
        out_specs=pl.BlockSpec((q, KS * CHUNK, LANES), lambda g: (0, g, 0)),
        out_shape=jax.ShapeDtypeStruct((q, fine_rows * KS, LANES), jnp.bfloat16),
        scratch_shapes=[
            pltpu.VMEM(((fine_rows + 2 * HB) * LANES, LANES), jnp.bfloat16),
            pltpu.VMEM((q * KS * CHUNK, LANES), jnp.float32),
        ],
        compiler_params=pltpu.CompilerParams(vmem_limit_bytes=40 * 1024 * 1024),
    )(a_tiles, near_p, code, group)


HALVES = 2
GROUP = 4
PIECE = 16
SPREAD = 40
AFTER = 2


def one_if(condition):
    return jnp.where(condition, 1.0, 0.0)


def halves_kernel(
    pair_count, devices,
    a_hbm, p_hbm, cols_hbm, group_hbm, slots_hbm, aggregate_hbm, out_ref,
    a_ref, p_ref, cols_ref, groups_ref, slots_ref, agg_ref,
    tiles, diag, turned, code, pick, stage, products, sums, term_ref, got, goals, sent_sums, got_sums, own_sums, final, parts,
    a_came, p_came, small_came, halo_sent, halo_came, sent, came, goal_sent, goal_came, cross_sent, cross_came, final_sent, final_came, self_came,
):
    q = BLK // 2
    me = lax.axis_index("rows") * pair_count + lax.axis_index("pair")
    team = devices // HALVES
    half, mine = lax.div(me, team), lax.rem(me, team)
    turn = half * (team // 2)
    mirror = me ^ (devices - team // 2)
    my_slice = mine ^ turn
    fine_rows = turned.shape[0] // BLK
    wide = term_ref.shape[2]
    chunks = fine_rows // PIECE
    coarse_rows = parts.shape[0] // KC
    members = team * KC
    ahead, behind = lax.rem(me + 1, devices), lax.rem(me + devices - 1, devices)

    def at(device):
        return (lax.div(device, pair_count), lax.rem(device, pair_count))

    def copy(src, dst, send_sem, recv_sem, device):
        return pltpu.make_async_remote_copy(
            src_ref=src,
            dst_ref=dst,
            send_sem=send_sem,
            recv_sem=recv_sem,
            device_id=at(device),
            device_id_type=pl.DeviceIdType.MESH,
        )

    def whole_rows(index, count):
        return pl.ds(pl.multiple_of(index * count, count), count)

    def a_copy(order):
        rows = whole_rows(lax.rem(order + 1, chunks), PIECE)
        return pltpu.make_async_copy(a_hbm.at[rows], a_ref.at[rows], a_came.at[order])

    def p_copy(t):
        rows = whole_rows(t, 8 * q)
        return pltpu.make_async_copy(p_hbm.at[rows], p_ref.at[rows], p_came.at[t])

    small = [
        pltpu.make_async_copy(src, dst, small_came.at[i])
        for i, (src, dst) in enumerate(
            [(cols_hbm, cols_ref), (group_hbm, groups_ref), (slots_hbm, slots_ref), (aggregate_hbm, agg_ref)]
        )
    ]
    edge = HB * LANES
    inner = fine_rows * LANES
    halo_up = copy(diag.at[pl.ds(inner, edge)], diag.at[pl.ds(0, edge)], halo_sent.at[0], halo_came.at[0], ahead)
    halo_down = copy(diag.at[pl.ds(edge, edge)], diag.at[pl.ds(inner + edge, edge)], halo_sent.at[1], halo_came.at[1], behind)

    def member(k):
        return mine ^ k

    def goal_copy(k, slot):
        return copy(goals.at[mine], goals.at[slot], goal_sent.at[k], goal_came.at[slot], half * team + member(k))

    def term_part(k, slot, chunk):
        rows = whole_rows(chunk, KS * PIECE)
        return copy(
            term_ref.at[member(k) ^ turn, rows], got.at[slot, rows], sent.at[k, chunk], came.at[slot, chunk], half * team + member(k)
        )

    def cross_copy(r):
        return copy(sent_sums.at[r], got_sums.at[r], cross_sent.at[r], cross_came.at[r], mirror)

    def final_copy(k, slot, r):
        lanes = pl.ds(pl.multiple_of((slot ^ turn) * wide, wide), wide)
        return copy(
            final.at[r, whole_rows(member(k), KC)],
            parts.at[whole_rows(r, KC), lanes],
            final_sent.at[k, r],
            final_came.at[slot, r],
            half * team + member(k),
        )

    barrier = pltpu.get_barrier_semaphore()
    for device in [half * team + member(k) for k in range(1, team)] + [mirror, ahead, behind]:
        pl.semaphore_signal(barrier, inc=1, device_id=at(device), device_id_type=pl.DeviceIdType.MESH)
    for t in range(fine_rows // 8):
        p_copy(t).start()
    for transfer in small:
        transfer.start()
    for order in range(chunks):
        a_copy(order).start()

    r128, k128 = iota((LANES, LANES), 0), iota((LANES, LANES), 1)
    want = one_if((r128 // BLK == k128 // BLK) & (r128 % BLK == 2 * (k128 % q) + (k128 // q) % 2)).astype(jnp.bfloat16)
    perm = one_if((r128 // BLK == k128 // BLK) & (k128 % BLK == 2 * (r128 % q) + (r128 % BLK) // q)).astype(jnp.bfloat16)
    low = iota((q, LANES), 1) < BLK

    for transfer in small:
        transfer.wait()
    offset = cols_ref[...] - (me * fine_rows + iota((KA, fine_rows), 1)) + HB
    for i in range(fine_rows):
        code[i] = jnp.broadcast_to(offset[:, i : i + 1], (KA, LANES))
    repeat = one_if(iota((KA, q * KA), 1) % KA == iota((KA, q * KA), 0)).astype(jnp.bfloat16)
    pick[...] = lax.dot_general(
        groups_ref[...].astype(jnp.float32).astype(jnp.bfloat16),
        repeat,
        (((0,), (0,)), ((), ())),
        preferred_element_type=jnp.float32,
    )
    count = fine_rows * KS
    term, fine = iota((fine_rows, count), 1), iota((fine_rows, count), 0)
    goal_rows = []
    for s in range(KS):
        place = one_if(term == (fine // PIECE) * (KS * PIECE) + s * PIECE + fine % PIECE).astype(jnp.bfloat16)
        values = jnp.concatenate(
            [
                jnp.broadcast_to(agg_ref[...], (KA, fine_rows)),
                jnp.broadcast_to(slots_ref[s : s + 1, :], (KA, fine_rows)),
            ],
            axis=0,
        )
        values = values.astype(jnp.float32).astype(jnp.bfloat16)
        goal_rows.append(jnp.dot(values, place, preferred_element_type=jnp.float32))
    goals[mine] = goal_rows[0] + goal_rows[1]

    def prepare(t8, _):
        p_copy(t8).wait()
        tiles[...] = p_ref[whole_rows(t8, 8 * q), :].astype(jnp.float32)
        for t2 in range(4):
            flats = []
            for u in range(2):
                flat = tiles[pl.ds(2 * t2 + u, q, stride=8), :]
                t = t8 * 8 + 2 * t2 + u
                diag[whole_rows(t + HB, LANES), :] = put_diagonal(flat, want, low)
                flats.append((flat, pltpu.roll(flat, BLK, 1)))
            both = jnp.concatenate(
                [jnp.where(low, flats[0][0], flats[1][1]), jnp.where(low, flats[0][1], flats[1][0])], axis=0
            ).astype(jnp.bfloat16)
            turned[whole_rows(t8 * 4 + t2, LANES), :] = lax.dot_general(
                perm, both, (((1,), (1,)), ((), ())), preferred_element_type=jnp.float32
            ).astype(jnp.bfloat16)
        return 0

    lax.fori_loop(0, fine_rows // 8, prepare, 0)
    pl.semaphore_wait(barrier, team + 2)
    halo_up.start()
    halo_down.start()
    for k in range(1, team):
        goal_copy(k, mine).start()

    even = one_if(iota((q, q * KA), 1) // KA == iota((q, q * KA), 0)).astype(jnp.bfloat16)

    def full_mask(condition):
        one = one_if(condition)
        pair = jnp.concatenate([one, one], axis=0).astype(jnp.bfloat16)
        return jnp.broadcast_to(pair[None], (q // 2,) + pair.shape).reshape(q * KA, LANES)

    def full(condition):
        return jnp.broadcast_to(condition[None], (q, KA, LANES)).reshape(q * KA, LANES)

    def multiply(first):
        for u2 in range(GROUP // 2):
            row = first + 2 * u2
            near = [diag[whole_rows(row + j, LANES), :] for j in range(NEAR + 1)]
            zero = jnp.zeros_like(near[0])
            middle = jnp.concatenate(
                [jnp.concatenate(near[1:3], axis=1), jnp.concatenate(near[3:5], axis=1)], axis=0
            )
            outer = jnp.concatenate(
                [jnp.concatenate([near[0], zero], axis=1), jnp.concatenate([zero, near[5]], axis=1)], axis=0
            )
            rows = [a_ref[row], a_ref[row + 1]]
            edges = jnp.dot(jnp.concatenate(rows, axis=1), outer, preferred_element_type=jnp.float32)
            for u in range(2):
                which = code[row + u] + u
                upper = rows[u] * full_mask((which == 3) | (which == 4))
                inside = jnp.dot(
                    jnp.concatenate([rows[u] - upper, upper], axis=1), middle, preferred_element_type=jnp.float32
                )
                result = jnp.where(
                    full(which == NEAR * u),
                    edges[:, u * LANES : (u + 1) * LANES],
                    jnp.where(full((which == 1) | (which == 3)), inside[:, :LANES], inside[:, LANES:]),
                )
                at_row = (2 * u2 + u) * q * KA
                products[at_row : at_row + q * KA, :] = result.astype(jnp.bfloat16)

    def add_groups(first):
        for u in range(GROUP):
            one = even * jnp.broadcast_to(pick[pl.ds(first + u, 1), :], even.shape).astype(jnp.bfloat16)
            both = jnp.dot(
                jnp.concatenate([even - one, one], axis=0),
                products[u * q * KA : (u + 1) * q * KA, :],
                preferred_element_type=jnp.float32,
            )
            s0, s1 = both[:q], both[q:]
            t0, t1 = pltpu.roll(s0, BLK, 1), pltpu.roll(s1, BLK, 1)
            sums[u * BLK : (u + 1) * BLK, :] = jnp.concatenate(
                [jnp.where(low, s0, t1), jnp.where(low, t0, s1)], axis=0
            ).astype(jnp.bfloat16)

    def project(first):
        for u in range(GROUP):
            row = first + u
            both = jnp.dot(
                turned[whole_rows(row, BLK), :],
                sums[u * BLK : (u + 1) * BLK, :],
                preferred_element_type=jnp.float32,
            )
            even_rows, odd_rows = both[:q], both[q:]
            t0, t1 = pltpu.roll(even_rows, BLK, 1), pltpu.roll(odd_rows, BLK, 1)
            place = lax.rem(row, PIECE)
            stage[pl.ds(place, q, stride=SPREAD), :] = jnp.where(low, even_rows, t1)
            stage[pl.ds(PIECE + place, q, stride=SPREAD), :] = jnp.where(low, t0, odd_rows)

    groups = fine_rows // GROUP
    per = PIECE // GROUP

    def first_row(index):
        return lax.rem(index + per, groups) * GROUP

    def step(t, _):
        @pl.when((lax.rem(t, per) == 0) & (t < groups))
        def _():
            a_copy(lax.div(t, per)).wait()

        @pl.when(t == (chunks - 2) * per)
        def _():
            halo_up.wait_recv()
            halo_down.wait_recv()

        project(first_row(jnp.maximum(t - 2, 0)))
        add_groups(first_row(jnp.clip(t - 1, 0, groups - 1)))
        multiply(first_row(jnp.minimum(t, groups - 1)))

        @pl.when((t >= AFTER) & (lax.rem(t - AFTER, per) == per - 1))
        def _():
            chunk = lax.rem(lax.div(t - AFTER, per) + 1, chunks)
            rows = whole_rows(chunk, KS * PIECE)
            for pair in range(q):
                lanes = slice(pair % 2 * LANES, pair % 2 * LANES + LANES)
                term_ref[pair // 2, rows, lanes] = stage[pair * SPREAD : pair * SPREAD + KS * PIECE, :].astype(jnp.bfloat16)
            for k in range(1, team):
                term_part(k, mine, chunk).start()

        return 0

    lax.fori_loop(0, groups + AFTER, step, 0)
    keep = pltpu.make_async_copy(term_ref.at[my_slice], got.at[mine], self_came)
    keep.start()
    for k in range(1, team):
        goal_copy(k, member(k)).wait_recv()
        for chunk in range(chunks):
            term_part(k, member(k), chunk).wait_recv()
    keep.wait()

    coarse = jnp.concatenate([goals[j, :KA] for j in range(team)], axis=1)
    slot = jnp.concatenate([goals[j, KA:] for j in range(team)], axis=1)
    slot = jnp.concatenate([slot, slot], axis=0)
    slot_hot = one_if(slot == iota(slot.shape, 0).astype(jnp.float32)).astype(jnp.bfloat16)

    def half_sums(which, r):
        pieces = []
        for j in range(team):
            row = ((which * team + j) * coarse_rows + r).astype(jnp.float32)
            one = one_if(coarse == row)
            pieces.append(slot_hot * jnp.concatenate([one, one], axis=0).astype(jnp.bfloat16))
        return jnp.dot(
            jnp.concatenate(pieces, axis=0), got[...].reshape(-1, wide), preferred_element_type=jnp.float32
        )

    def cross(r, _):
        sent_sums[r] = half_sums(1 - half, r).astype(jnp.bfloat16)
        cross_copy(r).start()
        return 0

    lax.fori_loop(0, coarse_rows, cross, 0)

    def keep_own(r, _):
        own_sums[r] = half_sums(half, r)
        return 0

    lax.fori_loop(0, coarse_rows, keep_own, 0)

    def finish(r, _):
        cross_copy(r).wait_recv()
        final[r] = (own_sums[r] + got_sums[r].astype(jnp.float32)).astype(jnp.bfloat16)
        for k in range(1, team):
            final_copy(k, mine, r).start()
        lanes = pl.ds(pl.multiple_of(my_slice * wide, wide), wide)
        parts[whole_rows(r, KC), lanes] = final[r, whole_rows(mine, KC), :]
        return 0

    lax.fori_loop(0, coarse_rows, finish, 0)

    def gather(r, _):
        for k in range(1, team):
            final_copy(k, member(k), r).wait_recv()
        out_ref[whole_rows(r, KC), :] = parts[whole_rows(r, KC), :].astype(jnp.float32)
        return 0

    lax.fori_loop(0, coarse_rows, gather, 0)
    halo_up.wait_send()
    halo_down.wait_send()
    for k in range(1, team):
        goal_copy(k, mine).wait_send()
        for chunk in range(chunks):
            term_part(k, mine, chunk).wait_send()
        for r in range(coarse_rows):
            final_copy(k, mine, r).wait_send()
    for r in range(coarse_rows):
        cross_copy(r).wait_send()


def by_halves(a_tiles, p_tiles, a_cols, tile_group, coarse_slots, aggregate):
    fine_rows, _, width = a_tiles.shape
    q = BLK // 2
    devices, pair_count = lax.axis_size(BOTH), lax.axis_size("pair")
    team = devices // HALVES
    wide = width // team
    count = fine_rows * KS
    coarse_rows = fine_rows // RATIO
    chunks = fine_rows // PIECE
    members = team * KC
    a = a_tiles.reshape(fine_rows, KA, q, LANES).transpose(0, 2, 1, 3).reshape(fine_rows, q * KA, LANES)
    p = p_tiles.reshape(fine_rows // 8, 8, q, LANES).transpose(0, 2, 1, 3).reshape(fine_rows * q, LANES)
    bf16, f32, i32 = jnp.bfloat16, jnp.float32, jnp.int32
    dma = pltpu.SemaphoreType.DMA
    return pl.pallas_call(
        functools.partial(halves_kernel, pair_count, devices),
        in_specs=[pl.BlockSpec(memory_space=pltpu.HBM)] * 6,
        out_specs=pl.BlockSpec(memory_space=pltpu.VMEM),
        out_shape=jax.ShapeDtypeStruct((coarse_rows * KC, width), f32),
        scratch_shapes=[
            pltpu.VMEM(a.shape, bf16),
            pltpu.VMEM(p.shape, bf16),
            pltpu.VMEM((KA, fine_rows), i32),
            pltpu.VMEM((KA, fine_rows), i32),
            pltpu.VMEM((KS, fine_rows), i32),
            pltpu.VMEM((1, fine_rows), i32),
            pltpu.VMEM((8 * q, LANES), f32),
            pltpu.VMEM(((fine_rows + 2 * HB) * LANES, LANES), bf16),
            pltpu.VMEM((fine_rows * BLK, BLK), bf16),
            pltpu.VMEM((fine_rows, KA, LANES), i32),
            pltpu.VMEM((fine_rows, q * KA), f32),
            pltpu.VMEM((q * SPREAD, LANES), f32),
            pltpu.VMEM((GROUP * q * KA, LANES), bf16),
            pltpu.VMEM((GROUP * BLK, LANES), bf16),
            pltpu.VMEM((team, count, wide), bf16),
            pltpu.VMEM((team, count, wide), bf16),
            pltpu.VMEM((team, 2 * KA, count), f32),
            pltpu.VMEM((coarse_rows, members, wide), bf16),
            pltpu.VMEM((coarse_rows, members, wide), bf16),
            pltpu.VMEM((coarse_rows, members, wide), f32),
            pltpu.VMEM((coarse_rows, members, wide), bf16),
            pltpu.VMEM((coarse_rows * KC, width), bf16),
            dma((chunks,)),
            dma((fine_rows // 8,)),
            dma((4,)),
            dma((2,)),
            dma((2,)),
            dma((team, chunks)),
            dma((team, chunks)),
            dma((team,)),
            dma((team,)),
            dma((coarse_rows,)),
            dma((coarse_rows,)),
            dma((team, coarse_rows)),
            dma((team, coarse_rows)),
            dma,
        ],
        compiler_params=pltpu.CompilerParams(
            collective_id=0, has_side_effects=True, vmem_limit_bytes=60 * 1024 * 1024
        ),
    )(a, p, a_cols.T, tile_group.T, coarse_slots.T, aggregate.reshape(1, fine_rows))


def routed(terms, coarse_slots, aggregate):
    fine_rows = aggregate.shape[0]
    q = BLK // 2
    width = BLK * BLK
    rows_count, pair_count = lax.axis_size("rows"), lax.axis_size("pair")
    flat = terms.reshape(q, fine_rows // CHUNK, KS, CHUNK, 2, BLK)
    flat = flat.transpose(1, 3, 2, 4, 0, 5).reshape(fine_rows, KS, width)
    group_size = fine_rows // RATIO * pair_count
    capacity = 2 * fine_rows // rows_count
    dest_group = aggregate // group_size
    local_rows = aggregate - dest_group * group_size
    targets = local_rows[:, None] * KC + coarse_slots
    order = jnp.arange(fine_rows)
    same = (dest_group[:, None] == dest_group[None, :]) & (order[None, :] < order[:, None])
    position = dest_group * capacity + jnp.sum(same.astype(jnp.int32), axis=1)

    def exchange(values):
        buffer = jnp.zeros((rows_count * capacity,) + values.shape[1:], values.dtype)
        buffer = buffer.at[position].set(values)
        return lax.all_to_all(buffer, "rows", split_axis=0, concat_axis=0, tiled=True)

    got = exchange(flat).reshape(-1, width).astype(jnp.float32)
    panel = jax.ops.segment_sum(
        got, exchange(targets).reshape(-1), num_segments=group_size * KC
    )
    panel = panel.reshape(group_size, KC, width)
    return lax.psum_scatter(panel, "pair", scatter_dimension=0, tiled=True)


def body(a_tiles, p_tiles, a_cols, tile_group, coarse_slots, aggregate):
    fine_rows, width = p_tiles.shape
    devices = lax.axis_size(BOTH)
    if devices * LANES != width:
        return routed(local_terms(a_tiles, p_tiles, a_cols, tile_group), coarse_slots, aggregate)
    result = by_halves(a_tiles, p_tiles, a_cols, tile_group, coarse_slots, aggregate)
    return result.reshape(fine_rows // RATIO, KC, width)


def solution(mesh):
    return jax.shard_map(
        body,
        mesh=mesh,
        in_specs=(
            P(BOTH, None, None),
            P(BOTH, None),
            P(BOTH, None),
            P(BOTH, None),
            P(BOTH, None),
            P(BOTH),
        ),
        out_specs=P(BOTH, None, None),
        check_vma=False,
    )
```

time: 57 us -> 60.6 us (1.063)
  Pallas kernels: 49.8 us -> 58.1 us
  local copies, waits for them, and re-layouts: 4.79 us -> 2.27 us
  other arithmetic: 2.04 us -> 0 us
    pallas_call x1, Pallas kernels: 49.8 us -> 58.1 us  [by_halves(): pl.pallas_call(functools.partial(halves_kernel, pair_count, devices), in_...]
    unnamed x6 -> x1, local copies, waits for them, and re-layouts: 4.3 us -> 2.27 us
    add x3 -> x0, other arithmetic: 1.37 us -> none  [the longest x1 0.69 us: row_codes(): offset = a_cols - own[:, None] + HB]
    mul x1 -> x0, other arithmetic: 0.67 us -> none  [body(): aggregate[:, None] * KC + coarse_slots]
where the time goes in v1:
time: 60.6 us; the launch traced here: 60.4 us
  Pallas kernels  58.1 us (96%)
  local copies, waits for them, and re-layouts  2.27 us (4%)
    pallas_call x1, Pallas kernels, by_halves(): pl.pallas_call(functools.partial(halves_kernel, pair_count, devices), in_...  58.1 us
    unnamed x1, local copies, waits for them, and re-layouts  2.27 us

profile of v1, /device:TPU:0, one launch (start us, length us, event | category | flops | bytes accessed | tf_op | source)
XLA Modules:
  0.0 60.4 jit_solution(10114287180855606350)
XLA Ops:
  0.0 58.1 %shard_map.64 = f32[64,4096]{1,0:T(8,128)} custom-call(bf16[64,256,128]{2,1,0:T(8,128)(2,1)} %bitcast.16, bf16[2048,128]{1,0:T(8,128)(2,1)} %bitcast.17, s32[8,64]{1,0:T(8,128)} %bitcast.18, s32[8,64]{1,0:T(8,128)} %bitcast.19, s32[2,64]{1,0:T(2,128)} %bitcast.20, s32[1,64]{1,0:T(1,128)} %bitcast.21), custom_call_target="tpu_custom_call" | custom-call | tf_op jit(solution)/shard_map/pallas_call | solution.py:498
  58.2 2.3 %copy.8 = f32[4,16,4096]{2,1,0:T(8,128)} copy(f32[4,16,4096]{2,1,0:T(8,128)} %bitcast.15) | data formatting | bytes 2097152

commit v2 on v1

--- a/solution.py
+++ b/solution.py
@@ -173,7 +173,7 @@
     a_hbm, p_hbm, cols_hbm, group_hbm, slots_hbm, aggregate_hbm, out_ref,
     a_ref, p_ref, cols_ref, groups_ref, slots_ref, agg_ref,
     tiles, diag, turned, code, pick, stage, products, sums, term_ref, got, goals, sent_sums, got_sums, own_sums, final, parts,
-    a_came, p_came, small_came, halo_sent, halo_came, sent, came, goal_sent, goal_came, cross_sent, cross_came, final_sent, final_came, self_came,
+    a_came, p_came, small_came, halo_sent, halo_came, sent, came, rest_sent, rest_came, goal_sent, goal_came, cross_sent, cross_came, final_sent, final_came, self_came,
 ):
     q = BLK // 2
     me = lax.axis_index("rows") * pair_count + lax.axis_index("pair")
@@ -183,7 +183,7 @@
     mirror = me ^ (devices - team // 2)
     my_slice = mine ^ turn
     fine_rows = turned.shape[0] // BLK
-    wide = term_ref.shape[2]
+    strips = got.shape[0]
     chunks = fine_rows // PIECE
     coarse_rows = parts.shape[0] // KC
     members = team * KC
@@ -230,22 +230,37 @@
     def goal_copy(k, slot):
         return copy(goals.at[mine], goals.at[slot], goal_sent.at[k], goal_came.at[slot], half * team + member(k))
 
+    def strip(slot, g):
+        return (slot ^ turn) * strips + g
+
     def term_part(k, slot, chunk):
         rows = whole_rows(chunk, KS * PIECE)
         return copy(
-            term_ref.at[member(k) ^ turn, rows], got.at[slot, rows], sent.at[k, chunk], came.at[slot, chunk], half * team + member(k)
-        )
-
-    def cross_copy(r):
-        return copy(sent_sums.at[r], got_sums.at[r], cross_sent.at[r], cross_came.at[r], mirror)
-
-    def final_copy(k, slot, r):
-        lanes = pl.ds(pl.multiple_of((slot ^ turn) * wide, wide), wide)
+            term_ref.at[strip(member(k), 0), rows],
+            got.at[0, slot, rows],
+            sent.at[k, chunk],
+            came.at[slot, chunk],
+            half * team + member(k),
+        )
+
+    def term_rest(k, slot, g):
         return copy(
-            final.at[r, whole_rows(member(k), KC)],
-            parts.at[whole_rows(r, KC), lanes],
-            final_sent.at[k, r],
-            final_came.at[slot, r],
+            term_ref.at[strip(member(k), g)],
+            got.at[g, slot],
+            rest_sent.at[k, g],
+            rest_came.at[slot, g],
+            half * team + member(k),
+        )
+
+    def cross_copy(g, r):
+        return copy(sent_sums.at[g, r], got_sums.at[g, r], cross_sent.at[g, r], cross_came.at[g, r], mirror)
+
+    def final_copy(k, slot, g, r):
+        return copy(
+            final.at[g, r, whole_rows(member(k), KC)],
+            parts.at[whole_rows(r, KC), whole_rows(strip(slot, g), LANES)],
+            final_sent.at[k, g, r],
+            final_came.at[slot, g, r],
             half * team + member(k),
         )
 
@@ -292,25 +307,26 @@
         goal_rows.append(jnp.dot(values, place, preferred_element_type=jnp.float32))
     goals[mine] = goal_rows[0] + goal_rows[1]
 
-    def prepare(t8, _):
-        p_copy(t8).wait()
-        tiles[...] = p_ref[whole_rows(t8, 8 * q), :].astype(jnp.float32)
-        for t2 in range(4):
+    def prepare(t16, _):
+        p_copy(2 * t16).wait()
+        p_copy(2 * t16 + 1).wait()
+        tiles[...] = p_ref[whole_rows(t16, 16 * q), :].astype(jnp.float32)
+        for t2 in range(8):
             flats = []
             for u in range(2):
-                flat = tiles[pl.ds(2 * t2 + u, q, stride=8), :]
-                t = t8 * 8 + 2 * t2 + u
+                flat = tiles[pl.ds(t2 // 4 * 8 * q + t2 % 4 * 2 + u, q, stride=8), :]
+                t = t16 * 16 + 2 * t2 + u
                 diag[whole_rows(t + HB, LANES), :] = put_diagonal(flat, want, low)
                 flats.append((flat, pltpu.roll(flat, BLK, 1)))
             both = jnp.concatenate(
                 [jnp.where(low, flats[0][0], flats[1][1]), jnp.where(low, flats[0][1], flats[1][0])], axis=0
             ).astype(jnp.bfloat16)
-            turned[whole_rows(t8 * 4 + t2, LANES), :] = lax.dot_general(
+            turned[whole_rows(t16 * 8 + t2, LANES), :] = lax.dot_general(
                 perm, both, (((1,), (1,)), ((), ())), preferred_element_type=jnp.float32
             ).astype(jnp.bfloat16)
         return 0
 
-    lax.fori_loop(0, fine_rows // 8, prepare, 0)
+    lax.fori_loop(0, fine_rows // 16, prepare, 0)
     pl.semaphore_wait(barrier, team + 2)
     halo_up.start()
     halo_down.start()
@@ -407,65 +423,74 @@
             chunk = lax.rem(lax.div(t - AFTER, per) + 1, chunks)
             rows = whole_rows(chunk, KS * PIECE)
             for pair in range(q):
-                lanes = slice(pair % 2 * LANES, pair % 2 * LANES + LANES)
-                term_ref[pair // 2, rows, lanes] = stage[pair * SPREAD : pair * SPREAD + KS * PIECE, :].astype(jnp.bfloat16)
+                term_ref[pair, rows, :] = stage[pair * SPREAD : pair * SPREAD + KS * PIECE, :].astype(jnp.bfloat16)
             for k in range(1, team):
                 term_part(k, mine, chunk).start()
 
         return 0
 
     lax.fori_loop(0, groups + AFTER, step, 0)
-    keep = pltpu.make_async_copy(term_ref.at[my_slice], got.at[mine], self_came)
-    keep.start()
+    for g in range(1, strips):
+        for k in range(1, team):
+            term_rest(k, mine, g).start()
+    keep = [pltpu.make_async_copy(term_ref.at[strip(mine, g)], got.at[g, mine], self_came.at[g]) for g in range(strips)]
+    for transfer in keep:
+        transfer.start()
     for k in range(1, team):
         goal_copy(k, member(k)).wait_recv()
         for chunk in range(chunks):
             term_part(k, member(k), chunk).wait_recv()
-    keep.wait()
 
     coarse = jnp.concatenate([goals[j, :KA] for j in range(team)], axis=1)
     slot = jnp.concatenate([goals[j, KA:] for j in range(team)], axis=1)
     slot = jnp.concatenate([slot, slot], axis=0)
     slot_hot = one_if(slot == iota(slot.shape, 0).astype(jnp.float32)).astype(jnp.bfloat16)
 
-    def half_sums(which, r):
+    def half_sums(which, g, r):
         pieces = []
         for j in range(team):
             row = ((which * team + j) * coarse_rows + r).astype(jnp.float32)
             one = one_if(coarse == row)
             pieces.append(slot_hot * jnp.concatenate([one, one], axis=0).astype(jnp.bfloat16))
         return jnp.dot(
-            jnp.concatenate(pieces, axis=0), got[...].reshape(-1, wide), preferred_element_type=jnp.float32
-        )
-
-    def cross(r, _):
-        sent_sums[r] = half_sums(1 - half, r).astype(jnp.bfloat16)
-        cross_copy(r).start()
-        return 0
-
-    lax.fori_loop(0, coarse_rows, cross, 0)
-
-    def keep_own(r, _):
-        own_sums[r] = half_sums(half, r)
-        return 0
-
-    lax.fori_loop(0, coarse_rows, keep_own, 0)
-
-    def finish(r, _):
-        cross_copy(r).wait_recv()
-        final[r] = (own_sums[r] + got_sums[r].astype(jnp.float32)).astype(jnp.bfloat16)
-        for k in range(1, team):
-            final_copy(k, mine, r).start()
-        lanes = pl.ds(pl.multiple_of(my_slice * wide, wide), wide)
-        parts[whole_rows(r, KC), lanes] = final[r, whole_rows(mine, KC), :]
-        return 0
-
-    lax.fori_loop(0, coarse_rows, finish, 0)
+            jnp.concatenate(pieces, axis=0), got[g].reshape(-1, LANES), preferred_element_type=jnp.float32
+        )
+
+    for g in range(strips):
+        keep[g].wait()
+        if g > 0:
+            for k in range(1, team):
+                term_rest(k, member(k), g).wait_recv()
+
+        def cross(r, _):
+            sent_sums[g, r] = half_sums(1 - half, g, r).astype(jnp.bfloat16)
+            cross_copy(g, r).start()
+            return 0
+
+        def keep_own(r, _):
+            own_sums[g, r] = half_sums(half, g, r)
+            return 0
+
+        lax.fori_loop(0, coarse_rows, cross, 0)
+        lax.fori_loop(0, coarse_rows, keep_own, 0)
+
+    for g in range(strips):
+
+        def finish(r, _):
+            cross_copy(g, r).wait_recv()
+            final[g, r] = (own_sums[g, r] + got_sums[g, r].astype(jnp.float32)).astype(jnp.bfloat16)
+            for k in range(1, team):
+                final_copy(k, mine, g, r).start()
+            parts[whole_rows(r, KC), whole_rows(strip(mine, g), LANES)] = final[g, r, whole_rows(mine, KC), :]
+            return 0
+
+        lax.fori_loop(0, coarse_rows, finish, 0)
 
     def gather(r, _):
-        for k in range(1, team):
-            final_copy(k, member(k), r).wait_recv()
-        out_ref[whole_rows(r, KC), :] = parts[whole_rows(r, KC), :].astype(jnp.float32)
+        for g in range(strips):
+            for k in range(1, team):
+                final_copy(k, member(k), g, r).wait_recv()
+        out_ref[whole_rows(r, KC), :] = parts[whole_rows(r, KC), :]
         return 0
 
     lax.fori_loop(0, coarse_rows, gather, 0)
@@ -475,10 +500,17 @@
         goal_copy(k, mine).wait_send()
         for chunk in range(chunks):
             term_part(k, mine, chunk).wait_send()
-        for r in range(coarse_rows):
-            final_copy(k, mine, r).wait_send()
-    for r in range(coarse_rows):
-        cross_copy(r).wait_send()
+        for g in range(1, strips):
+            term_rest(k, mine, g).wait_send()
+
+    def sent_all(r, _):
+        for g in range(strips):
+            cross_copy(g, r).wait_send()
+            for k in range(1, team):
+                final_copy(k, mine, g, r).wait_send()
+        return 0
+
+    lax.fori_loop(0, coarse_rows, sent_all, 0)
 
 
 def by_halves(a_tiles, p_tiles, a_cols, tile_group, coarse_slots, aggregate):
@@ -486,7 +518,7 @@
     q = BLK // 2
     devices, pair_count = lax.axis_size(BOTH), lax.axis_size("pair")
     team = devices // HALVES
-    wide = width // team
+    strips = width // team // LANES
     count = fine_rows * KS
     coarse_rows = fine_rows // RATIO
     chunks = fine_rows // PIECE
@@ -499,7 +531,7 @@
         functools.partial(halves_kernel, pair_count, devices),
         in_specs=[pl.BlockSpec(memory_space=pltpu.HBM)] * 6,
         out_specs=pl.BlockSpec(memory_space=pltpu.VMEM),
-        out_shape=jax.ShapeDtypeStruct((coarse_rows * KC, width), f32),
+        out_shape=jax.ShapeDtypeStruct((coarse_rows * KC, width), bf16),
         scratch_shapes=[
             pltpu.VMEM(a.shape, bf16),
             pltpu.VMEM(p.shape, bf16),
@@ -507,7 +539,7 @@
             pltpu.VMEM((KA, fine_rows), i32),
             pltpu.VMEM((KS, fine_rows), i32),
             pltpu.VMEM((1, fine_rows), i32),
-            pltpu.VMEM((8 * q, LANES), f32),
+            pltpu.VMEM((16 * q, LANES), f32),
             pltpu.VMEM(((fine_rows + 2 * HB) * LANES, LANES), bf16),
             pltpu.VMEM((fine_rows * BLK, BLK), bf16),
             pltpu.VMEM((fine_rows, KA, LANES), i32),
@@ -515,13 +547,13 @@
             pltpu.VMEM((q * SPREAD, LANES), f32),
             pltpu.VMEM((GROUP * q * KA, LANES), bf16),
             pltpu.VMEM((GROUP * BLK, LANES), bf16),
-            pltpu.VMEM((team, count, wide), bf16),
-            pltpu.VMEM((team, count, wide), bf16),
+            pltpu.VMEM((width // LANES, count, LANES), bf16),
+            pltpu.VMEM((strips, team, count, LANES), bf16),
             pltpu.VMEM((team, 2 * KA, count), f32),
-            pltpu.VMEM((coarse_rows, members, wide), bf16),
-            pltpu.VMEM((coarse_rows, members, wide), bf16),
-            pltpu.VMEM((coarse_rows, members, wide), f32),
-            pltpu.VMEM((coarse_rows, members, wide), bf16),
+            pltpu.VMEM((strips, coarse_rows, members, LANES), bf16),
+            pltpu.VMEM((strips, coarse_rows, members, LANES), bf16),
+            pltpu.VMEM((strips, coarse_rows, members, LANES), f32),
+            pltpu.VMEM((strips, coarse_rows, members, LANES), bf16),
             pltpu.VMEM((coarse_rows * KC, width), bf16),
             dma((chunks,)),
             dma((fine_rows // 8,)),
@@ -530,13 +562,15 @@
             dma((2,)),
             dma((team, chunks)),
             dma((team, chunks)),
+            dma((team, strips)),
+            dma((team, strips)),
             dma((team,)),
             dma((team,)),
-            dma((coarse_rows,)),
-            dma((coarse_rows,)),
-            dma((team, coarse_rows)),
-            dma((team, coarse_rows)),
-            dma,
+            dma((strips, coarse_rows)),
+            dma((strips, coarse_rows)),
+            dma((team, strips, coarse_rows)),
+            dma((team, strips, coarse_rows)),
+            dma((strips,)),
         ],
         compiler_params=pltpu.CompilerParams(
             collective_id=0, has_side_effects=True, vmem_limit_bytes=60 * 1024 * 1024
@@ -579,7 +613,7 @@
     if devices * LANES != width:
         return routed(local_terms(a_tiles, p_tiles, a_cols, tile_group), coarse_slots, aggregate)
     result = by_halves(a_tiles, p_tiles, a_cols, tile_group, coarse_slots, aggregate)
-    return result.reshape(fine_rows // RATIO, KC, width)
+    return result.reshape(fine_rows // RATIO, KC, width).astype(jnp.float32)
 
 
 def solution(mesh):

time: 60.6 us -> 58.2 us (0.960)
  local copies, waits for them, and re-layouts: 2.27 us -> 0 us
  Pallas kernels: 58.1 us -> 55.9 us
  other arithmetic: 0 us -> 2.08 us
    unnamed x1 -> x0, local copies, waits for them, and re-layouts: 2.27 us -> none
    pallas_call x1, Pallas kernels: 58.1 us -> 55.9 us  [by_halves(): pl.pallas_call(functools.partial(halves_kernel, pair_count, devices), in_...]
    convert_element_type x0 -> x1, other arithmetic: none -> 2.08 us  [body(): return result.reshape(fine_rows // RATIO, KC, width).astype(jnp.float32)]
where the time goes in v2:
time: 58.2 us; the launch traced here: 58 us
  Pallas kernels  55.9 us (96%)
  other arithmetic  2.08 us (4%)
    pallas_call x1, Pallas kernels, by_halves(): pl.pallas_call(functools.partial(halves_kernel, pair_count, devices), in_...  55.9 us
    convert_element_type x1, other arithmetic, body(): return result.reshape(fine_rows // RATIO, KC, width).astype(jnp.float32)  2.08 us

profile of v2, /device:TPU:0, one launch (start us, length us, event | category | flops | bytes accessed | tf_op | source)
XLA Modules:
  0.0 58.0 jit_solution(18353617691438366697)
XLA Ops:
  0.0 55.9 %shard_map.64 = bf16[64,4096]{1,0:T(8,128)(2,1)} custom-call(bf16[64,256,128]{2,1,0:T(8,128)(2,1)} %bitcast.16, bf16[2048,128]{1,0:T(8,128)(2,1)} %bitcast.18, s32[8,64]{1,0:T(8,128)} %bitcast.19, s32[8,64]{1,0:T(8,128)} %bitcast.20, s32[2,64]{1,0:T(2,128)} %bitcast.21, s32[1,64]{1,0:T(1,128)} %bitcast.22), custom_call_target="tpu_custom_call" | custom-call | tf_op jit(solution)/shard_map/pallas_call | solution.py:530
  55.9 2.1 %convert.1 = f32[4,16,4096]{2,1,0:T(8,128)} convert(bf16[4,16,4096]{2,1,0:T(8,128)(2,1)} %bitcast.17) | non-fusion elementwise | flops 262144 | bytes 1572864 | tf_op jit(solution)/shard_map/convert_element_type | solution.py:616

commit v3 on v2

--- a/solution.py
+++ b/solution.py
@@ -162,6 +162,7 @@
 PIECE = 16
 SPREAD = 40
 AFTER = 2
+FLIGHT = 2
 
 
 def one_if(condition):
@@ -172,8 +173,8 @@
     pair_count, devices,
     a_hbm, p_hbm, cols_hbm, group_hbm, slots_hbm, aggregate_hbm, out_ref,
     a_ref, p_ref, cols_ref, groups_ref, slots_ref, agg_ref,
-    tiles, diag, turned, code, pick, stage, products, sums, term_ref, got, goals, sent_sums, got_sums, own_sums, final, parts,
-    a_came, p_came, small_came, halo_sent, halo_came, sent, came, rest_sent, rest_came, goal_sent, goal_came, cross_sent, cross_came, final_sent, final_came, self_came,
+    tiles, diag, turned, code, pick, stage, products, sums, term_ref, got, goals, sent_sums, got_sums, final, parts,
+    a_came, p_came, small_came, halo_sent, halo_came, sent, came, goal_sent, goal_came, cross_sent, cross_came, final_sent, final_came, self_came,
 ):
     q = BLK // 2
     me = lax.axis_index("rows") * pair_count + lax.axis_index("pair")
@@ -227,42 +228,37 @@
     def member(k):
         return mine ^ k
 
-    def goal_copy(k, slot):
-        return copy(goals.at[mine], goals.at[slot], goal_sent.at[k], goal_came.at[slot], half * team + member(k))
+    def goal_copy(k):
+        return copy(goals.at[mine], goals.at[mine], goal_sent, goal_came, half * team + member(k))
 
     def strip(slot, g):
         return (slot ^ turn) * strips + g
 
-    def term_part(k, slot, chunk):
+    def term_part(k, chunk):
         rows = whole_rows(chunk, KS * PIECE)
+        return copy(term_ref.at[strip(member(k), 0), rows], got.at[0, mine, rows], sent.at[0], came.at[0], half * team + member(k))
+
+    def term_rest(k, g):
+        return copy(term_ref.at[strip(member(k), g)], got.at[g, mine], sent.at[g], came.at[g], half * team + member(k))
+
+    def cross_copy(n):
+        return copy(sent_sums.at[n], got_sums.at[n], cross_sent.at[n], cross_came.at[n], mirror)
+
+    def final_copy(k, n):
+        g, r = lax.div(n, coarse_rows), lax.rem(n, coarse_rows)
         return copy(
-            term_ref.at[strip(member(k), 0), rows],
-            got.at[0, slot, rows],
-            sent.at[k, chunk],
-            came.at[slot, chunk],
+            final.at[n, whole_rows(member(k), KC)],
+            parts.at[whole_rows(r, KC), whole_rows(strip(mine, g), LANES)],
+            final_sent,
+            final_came,
             half * team + member(k),
         )
 
-    def term_rest(k, slot, g):
-        return copy(
-            term_ref.at[strip(member(k), g)],
-            got.at[g, slot],
-            rest_sent.at[k, g],
-            rest_came.at[slot, g],
-            half * team + member(k),
-        )
-
-    def cross_copy(g, r):
-        return copy(sent_sums.at[g, r], got_sums.at[g, r], cross_sent.at[g, r], cross_came.at[g, r], mirror)
-
-    def final_copy(k, slot, g, r):
-        return copy(
-            final.at[g, r, whole_rows(member(k), KC)],
-            parts.at[whole_rows(r, KC), whole_rows(strip(slot, g), LANES)],
-            final_sent.at[k, g, r],
-            final_came.at[slot, g, r],
-            half * team + member(k),
-        )
+    others = pl.ds(0, team - 1)
+    all_goals = copy(goals.at[others], goals.at[others], goal_sent, goal_came, mirror)
+    all_terms = [copy(got.at[g, others], got.at[g, others], sent.at[g], came.at[g], mirror) for g in range(strips)]
+    but_one = pl.ds(0, members - KC)
+    all_final = copy(final.at[:, but_one], final.at[:, but_one], final_sent, final_came, mirror)
 
     barrier = pltpu.get_barrier_semaphore()
     for device in [half * team + member(k) for k in range(1, team)] + [mirror, ahead, behind]:
@@ -296,12 +292,10 @@
     goal_rows = []
     for s in range(KS):
         place = one_if(term == (fine // PIECE) * (KS * PIECE) + s * PIECE + fine % PIECE).astype(jnp.bfloat16)
-        values = jnp.concatenate(
-            [
-                jnp.broadcast_to(agg_ref[...], (KA, fine_rows)),
-                jnp.broadcast_to(slots_ref[s : s + 1, :], (KA, fine_rows)),
-            ],
-            axis=0,
+        values = jnp.where(
+            iota((KA, fine_rows), 0) == 0,
+            jnp.broadcast_to(agg_ref[...], (KA, fine_rows)),
+            jnp.broadcast_to(slots_ref[s : s + 1, :], (KA, fine_rows)),
         )
         values = values.astype(jnp.float32).astype(jnp.bfloat16)
         goal_rows.append(jnp.dot(values, place, preferred_element_type=jnp.float32))
@@ -331,7 +325,7 @@
     halo_up.start()
     halo_down.start()
     for k in range(1, team):
-        goal_copy(k, mine).start()
+        goal_copy(k).start()
 
     even = one_if(iota((q, q * KA), 1) // KA == iota((q, q * KA), 0)).astype(jnp.bfloat16)
 
@@ -425,28 +419,30 @@
             for pair in range(q):
                 term_ref[pair, rows, :] = stage[pair * SPREAD : pair * SPREAD + KS * PIECE, :].astype(jnp.bfloat16)
             for k in range(1, team):
-                term_part(k, mine, chunk).start()
+                term_part(k, chunk).start()
 
         return 0
 
     lax.fori_loop(0, groups + AFTER, step, 0)
     for g in range(1, strips):
         for k in range(1, team):
-            term_rest(k, mine, g).start()
+            term_rest(k, g).start()
     keep = [pltpu.make_async_copy(term_ref.at[strip(mine, g)], got.at[g, mine], self_came.at[g]) for g in range(strips)]
     for transfer in keep:
         transfer.start()
-    for k in range(1, team):
-        goal_copy(k, member(k)).wait_recv()
-        for chunk in range(chunks):
-            term_part(k, member(k), chunk).wait_recv()
-
-    coarse = jnp.concatenate([goals[j, :KA] for j in range(team)], axis=1)
-    slot = jnp.concatenate([goals[j, KA:] for j in range(team)], axis=1)
-    slot = jnp.concatenate([slot, slot], axis=0)
+    all_goals.wait_recv()
+    all_terms[0].wait_recv()
+    keep[0].wait()
+
+    def everyone(row, copies):
+        return jnp.concatenate([jnp.broadcast_to(goals[j, row : row + 1, :], (copies, count)) for j in range(team)], axis=1)
+
+    coarse = everyone(0, KA)
+    slot = everyone(1, 2 * KA)
     slot_hot = one_if(slot == iota(slot.shape, 0).astype(jnp.float32)).astype(jnp.bfloat16)
 
-    def half_sums(which, g, r):
+    def half_sums(which, n):
+        g, r = lax.div(n, coarse_rows), lax.rem(n, coarse_rows)
         pieces = []
         for j in range(team):
             row = ((which * team + j) * coarse_rows + r).astype(jnp.float32)
@@ -456,61 +452,56 @@
             jnp.concatenate(pieces, axis=0), got[g].reshape(-1, LANES), preferred_element_type=jnp.float32
         )
 
-    for g in range(strips):
-        keep[g].wait()
-        if g > 0:
-            for k in range(1, team):
-                term_rest(k, member(k), g).wait_recv()
-
-        def cross(r, _):
-            sent_sums[g, r] = half_sums(1 - half, g, r).astype(jnp.bfloat16)
-            cross_copy(g, r).start()
-            return 0
-
-        def keep_own(r, _):
-            own_sums[g, r] = half_sums(half, g, r)
-            return 0
-
-        lax.fori_loop(0, coarse_rows, cross, 0)
-        lax.fori_loop(0, coarse_rows, keep_own, 0)
-
-    for g in range(strips):
-
-        def finish(r, _):
-            cross_copy(g, r).wait_recv()
-            final[g, r] = (own_sums[g, r] + got_sums[g, r].astype(jnp.float32)).astype(jnp.bfloat16)
-            for k in range(1, team):
-                final_copy(k, mine, g, r).start()
-            parts[whole_rows(r, KC), whole_rows(strip(mine, g), LANES)] = final[g, r, whole_rows(mine, KC), :]
-            return 0
-
-        lax.fori_loop(0, coarse_rows, finish, 0)
-
-    def gather(r, _):
-        for g in range(strips):
-            for k in range(1, team):
-                final_copy(k, member(k), g, r).wait_recv()
-        out_ref[whole_rows(r, KC), :] = parts[whole_rows(r, KC), :]
+    steps = strips * coarse_rows
+
+    def cross(n, _):
+        sent_sums[n] = half_sums(1 - half, n).astype(jnp.bfloat16)
+
+        @pl.when(n < FLIGHT)
+        def _():
+            cross_copy(n).start()
+
         return 0
 
-    lax.fori_loop(0, coarse_rows, gather, 0)
+    lax.fori_loop(0, FLIGHT, cross, 0)
+
+    def finish(n, _):
+        @pl.when(n == coarse_rows - FLIGHT)
+        def _():
+            for g in range(1, strips):
+                all_terms[g].wait_recv()
+                keep[g].wait()
+
+        @pl.when(n < steps - FLIGHT)
+        def _():
+            cross(n + FLIGHT, 0)
+
+        own = half_sums(half, n)
+
+        @pl.when(n < steps - FLIGHT)
+        def _():
+            cross_copy(n).wait_send()
+            cross_copy(n + FLIGHT).start()
+
+        cross_copy(n).wait_recv()
+        final[n] = (own + got_sums[n].astype(jnp.float32)).astype(jnp.bfloat16)
+        for k in range(1, team):
+            final_copy(k, n).start()
+        g, r = lax.div(n, coarse_rows), lax.rem(n, coarse_rows)
+        parts[whole_rows(r, KC), whole_rows(strip(mine, g), LANES)] = final[n, whole_rows(mine, KC), :]
+        return 0
+
+    lax.fori_loop(0, steps, finish, 0)
     halo_up.wait_send()
     halo_down.wait_send()
-    for k in range(1, team):
-        goal_copy(k, mine).wait_send()
-        for chunk in range(chunks):
-            term_part(k, mine, chunk).wait_send()
-        for g in range(1, strips):
-            term_rest(k, mine, g).wait_send()
-
-    def sent_all(r, _):
-        for g in range(strips):
-            cross_copy(g, r).wait_send()
-            for k in range(1, team):
-                final_copy(k, mine, g, r).wait_send()
-        return 0
-
-    lax.fori_loop(0, coarse_rows, sent_all, 0)
+    all_goals.wait_send()
+    for g in range(strips):
+        all_terms[g].wait_send()
+    for n in range(steps - FLIGHT, steps):
+        cross_copy(n).wait_send()
+    all_final.wait_send()
+    all_final.wait_recv()
+    out_ref[...] = parts[...]
 
 
 def by_halves(a_tiles, p_tiles, a_cols, tile_group, coarse_slots, aggregate):
@@ -549,27 +540,24 @@
             pltpu.VMEM((GROUP * BLK, LANES), bf16),
             pltpu.VMEM((width // LANES, count, LANES), bf16),
             pltpu.VMEM((strips, team, count, LANES), bf16),
-            pltpu.VMEM((team, 2 * KA, count), f32),
-            pltpu.VMEM((strips, coarse_rows, members, LANES), bf16),
-            pltpu.VMEM((strips, coarse_rows, members, LANES), bf16),
-            pltpu.VMEM((strips, coarse_rows, members, LANES), f32),
-            pltpu.VMEM((strips, coarse_rows, members, LANES), bf16),
+            pltpu.VMEM((team, KA, count), f32),
+            pltpu.VMEM((strips * coarse_rows, members, LANES), bf16),
+            pltpu.VMEM((strips * coarse_rows, members, LANES), bf16),
+            pltpu.VMEM((strips * coarse_rows, members, LANES), bf16),
             pltpu.VMEM((coarse_rows * KC, width), bf16),
             dma((chunks,)),
             dma((fine_rows // 8,)),
             dma((4,)),
             dma((2,)),
             dma((2,)),
-            dma((team, chunks)),
-            dma((team, chunks)),
-            dma((team, strips)),
-            dma((team, strips)),
-            dma((team,)),
-            dma((team,)),
-            dma((strips, coarse_rows)),
-            dma((strips, coarse_rows)),
-            dma((team, strips, coarse_rows)),
-            dma((team, strips, coarse_rows)),
+            dma((strips,)),
+            dma((strips,)),
+            dma,
+            dma,
+            dma((strips * coarse_rows,)),
+            dma((strips * coarse_rows,)),
+            dma,
+            dma,
             dma((strips,)),
         ],
         compiler_params=pltpu.CompilerParams(

time: 58.2 us -> 55 us (0.945)
  Pallas kernels: 55.9 us -> 52.8 us
    pallas_call x1, Pallas kernels: 55.9 us -> 52.8 us  [by_halves(): pl.pallas_call(functools.partial(halves_kernel, pair_count, devices), in_...]
where the time goes in v3:
time: 55 us; the launch traced here: 54.9 us
  Pallas kernels  52.8 us (96%)
  other arithmetic  2.08 us (4%)
    pallas_call x1, Pallas kernels, by_halves(): pl.pallas_call(functools.partial(halves_kernel, pair_count, devices), in_...  52.8 us
    convert_element_type x1, other arithmetic, body(): return result.reshape(fine_rows // RATIO, KC, width).astype(jnp.float32)  2.08 us

profile of v3, /device:TPU:0, one launch (start us, length us, event | category | flops | bytes accessed | tf_op | source)
XLA Modules:
  0.0 54.9 jit_solution(18221092650451989641)
XLA Ops:
  0.0 52.8 %shard_map.64 = bf16[64,4096]{1,0:T(8,128)(2,1)} custom-call(bf16[64,256,128]{2,1,0:T(8,128)(2,1)} %bitcast.16, bf16[2048,128]{1,0:T(8,128)(2,1)} %bitcast.18, s32[8,64]{1,0:T(8,128)} %bitcast.19, s32[8,64]{1,0:T(8,128)} %bitcast.20, s32[2,64]{1,0:T(2,128)} %bitcast.21, s32[1,64]{1,0:T(1,128)} %bitcast.22), custom_call_target="tpu_custom_call" | custom-call | tf_op jit(solution)/shard_map/pallas_call | solution.py:521
  52.8 2.1 %convert.1 = f32[4,16,4096]{2,1,0:T(8,128)} convert(bf16[4,16,4096]{2,1,0:T(8,128)(2,1)} %bitcast.17) | non-fusion elementwise | flops 262144 | bytes 1572864 | tf_op jit(solution)/shard_map/convert_element_type | solution.py:604

commit v4 on v3

--- a/solution.py
+++ b/solution.py
@@ -162,7 +162,7 @@
 PIECE = 16
 SPREAD = 40
 AFTER = 2
-FLIGHT = 2
+FLIGHT = 3
 
 
 def one_if(condition):
@@ -186,7 +186,7 @@
     fine_rows = turned.shape[0] // BLK
     strips = got.shape[0]
     chunks = fine_rows // PIECE
-    coarse_rows = parts.shape[0] // KC
+    coarse_rows = parts.shape[1] // KC
     members = team * KC
     ahead, behind = lax.rem(me + 1, devices), lax.rem(me + devices - 1, devices)
 
@@ -244,21 +244,27 @@
     def cross_copy(n):
         return copy(sent_sums.at[n], got_sums.at[n], cross_sent.at[n], cross_came.at[n], mirror)
 
-    def final_copy(k, n):
-        g, r = lax.div(n, coarse_rows), lax.rem(n, coarse_rows)
+    held = coarse_rows * KC
+    batch = members // held
+    batches = team // batch
+
+    def first_owner(n):
+        return lax.rem(lax.rem(n, batches) + my_slice, batches) * batch
+
+    def final_copy(n, b):
         return copy(
-            final.at[n, whole_rows(member(k), KC)],
-            parts.at[whole_rows(r, KC), whole_rows(strip(mine, g), LANES)],
+            final.at[n, whole_rows(b, held)],
+            parts.at[strip(mine, lax.div(n, batches))],
             final_sent,
             final_came,
-            half * team + member(k),
+            half * team + first_owner(n) + b,
         )
 
     others = pl.ds(0, team - 1)
     all_goals = copy(goals.at[others], goals.at[others], goal_sent, goal_came, mirror)
     all_terms = [copy(got.at[g, others], got.at[g, others], sent.at[g], came.at[g], mirror) for g in range(strips)]
-    but_one = pl.ds(0, members - KC)
-    all_final = copy(final.at[:, but_one], final.at[:, but_one], final_sent, final_came, mirror)
+    but_own = pl.ds(0, strips * (team - 1))
+    all_final = copy(parts.at[but_own], parts.at[but_own], final_sent, final_came, mirror)
 
     barrier = pltpu.get_barrier_semaphore()
     for device in [half * team + member(k) for k in range(1, team)] + [mirror, ahead, behind]:
@@ -442,17 +448,16 @@
     slot_hot = one_if(slot == iota(slot.shape, 0).astype(jnp.float32)).astype(jnp.bfloat16)
 
     def half_sums(which, n):
-        g, r = lax.div(n, coarse_rows), lax.rem(n, coarse_rows)
+        first = (which * team + first_owner(n)) * coarse_rows
         pieces = []
-        for j in range(team):
-            row = ((which * team + j) * coarse_rows + r).astype(jnp.float32)
-            one = one_if(coarse == row)
+        for j in range(batch * coarse_rows):
+            one = one_if(coarse == (first + j).astype(jnp.float32))
             pieces.append(slot_hot * jnp.concatenate([one, one], axis=0).astype(jnp.bfloat16))
         return jnp.dot(
-            jnp.concatenate(pieces, axis=0), got[g].reshape(-1, LANES), preferred_element_type=jnp.float32
+            jnp.concatenate(pieces, axis=0), got[lax.div(n, batches)].reshape(-1, LANES), preferred_element_type=jnp.float32
         )
 
-    steps = strips * coarse_rows
+    steps = strips * batches
 
     def cross(n, _):
         sent_sums[n] = half_sums(1 - half, n).astype(jnp.bfloat16)
@@ -466,7 +471,7 @@
     lax.fori_loop(0, FLIGHT, cross, 0)
 
     def finish(n, _):
-        @pl.when(n == coarse_rows - FLIGHT)
+        @pl.when(n == batches - FLIGHT)
         def _():
             for g in range(1, strips):
                 all_terms[g].wait_recv()
@@ -485,10 +490,17 @@
 
         cross_copy(n).wait_recv()
         final[n] = (own + got_sums[n].astype(jnp.float32)).astype(jnp.bfloat16)
-        for k in range(1, team):
-            final_copy(k, n).start()
-        g, r = lax.div(n, coarse_rows), lax.rem(n, coarse_rows)
-        parts[whole_rows(r, KC), whole_rows(strip(mine, g), LANES)] = final[n, whole_rows(mine, KC), :]
+        for b in range(batch):
+            owner = first_owner(n) + b
+
+            @pl.when(owner != mine)
+            def _():
+                final_copy(n, b).start()
+
+            @pl.when(owner == mine)
+            def _():
+                parts[strip(mine, lax.div(n, batches))] = final[n, b * held : (b + 1) * held, :]
+
         return 0
 
     lax.fori_loop(0, steps, finish, 0)
@@ -501,7 +513,8 @@
         cross_copy(n).wait_send()
     all_final.wait_send()
     all_final.wait_recv()
-    out_ref[...] = parts[...]
+    for column in range(parts.shape[0]):
+        out_ref[:, column * LANES : (column + 1) * LANES] = parts[column]
 
 
 def by_halves(a_tiles, p_tiles, a_cols, tile_group, coarse_slots, aggregate):
@@ -544,7 +557,7 @@
             pltpu.VMEM((strips * coarse_rows, members, LANES), bf16),
             pltpu.VMEM((strips * coarse_rows, members, LANES), bf16),
             pltpu.VMEM((strips * coarse_rows, members, LANES), bf16),
-            pltpu.VMEM((coarse_rows * KC, width), bf16),
+            pltpu.VMEM((width // LANES, coarse_rows * KC, LANES), bf16),
             dma((chunks,)),
             dma((fine_rows // 8,)),
             dma((4,)),

time: 55 us -> 52.4 us (0.953)
  Pallas kernels: 52.8 us -> 50.2 us
    pallas_call x1, Pallas kernels: 52.8 us -> 50.2 us  [by_halves(): pl.pallas_call(functools.partial(halves_kernel, pair_count, devices), in_...]
where the time goes in v4:
time: 52.4 us; the launch traced here: 52.3 us
  Pallas kernels  50.2 us (96%)
  other arithmetic  2.08 us (4%)
    pallas_call x1, Pallas kernels, by_halves(): pl.pallas_call(functools.partial(halves_kernel, pair_count, devices), in_...  50.2 us
    convert_element_type x1, other arithmetic, body(): return result.reshape(fine_rows // RATIO, KC, width).astype(jnp.float32)  2.08 us

profile of v4, /device:TPU:0, one launch (start us, length us, event | category | flops | bytes accessed | tf_op | source)
XLA Modules:
  0.0 52.3 jit_solution(11293977423844317166)
XLA Ops:
  0.0 50.2 %shard_map.64 = bf16[64,4096]{1,0:T(8,128)(2,1)} custom-call(bf16[64,256,128]{2,1,0:T(8,128)(2,1)} %bitcast.16, bf16[2048,128]{1,0:T(8,128)(2,1)} %bitcast.18, s32[8,64]{1,0:T(8,128)} %bitcast.19, s32[8,64]{1,0:T(8,128)} %bitcast.20, s32[2,64]{1,0:T(2,128)} %bitcast.21, s32[1,64]{1,0:T(1,128)} %bitcast.22), custom_call_target="tpu_custom_call" | custom-call | tf_op jit(solution)/shard_map/pallas_call | solution.py:534
  50.2 2.1 %convert.1 = f32[4,16,4096]{2,1,0:T(8,128)} convert(bf16[4,16,4096]{2,1,0:T(8,128)(2,1)} %bitcast.17) | non-fusion elementwise | flops 262144 | bytes 1572864 | tf_op jit(solution)/shard_map/convert_element_type | solution.py:617

commit v5 on v4

--- a/solution.py
+++ b/solution.py
@@ -163,6 +163,7 @@
 SPREAD = 40
 AFTER = 2
 FLIGHT = 3
+SHARE = 2
 
 
 def one_if(condition):
@@ -173,8 +174,8 @@
     pair_count, devices,
     a_hbm, p_hbm, cols_hbm, group_hbm, slots_hbm, aggregate_hbm, out_ref,
     a_ref, p_ref, cols_ref, groups_ref, slots_ref, agg_ref,
-    tiles, diag, turned, code, pick, stage, products, sums, term_ref, got, goals, sent_sums, got_sums, final, parts,
-    a_came, p_came, small_came, halo_sent, halo_came, sent, came, goal_sent, goal_came, cross_sent, cross_came, final_sent, final_came, self_came,
+    tiles, diag, turned, code, pick, stage, products, sums, term_ref, got, goals, sent_sums, got_sums, final, parts, far, far_goals, own,
+    a_came, p_came, small_came, halo_sent, halo_came, sent, came, goal_sent, goal_came, cross_sent, cross_came, final_sent, final_came, self_came, far_sent, far_came, far_goal_sent, far_goal_came,
 ):
     q = BLK // 2
     me = lax.axis_index("rows") * pair_count + lax.axis_index("pair")
@@ -260,6 +261,25 @@
             half * team + first_owner(n) + b,
         )
 
+    holders = team // SHARE
+    both_hold = lax.rem(mine, SHARE) == 0
+    far_team = (1 - half) * team
+
+    def far_part(h, chunk):
+        rows = whole_rows(chunk, KS * PIECE)
+        to = lax.rem(h * SHARE + mine, team) // SHARE * SHARE
+        place = (to ^ (team // 2 - turn)) * strips
+        return copy(term_ref.at[place, rows], far.at[mine, rows], far_sent, far_came, far_team + to)
+
+    def far_goal(h):
+        return copy(goals.at[mine], far_goals.at[mine], far_goal_sent, far_goal_came, far_team + h * SHARE)
+
+    some = pl.ds(0, holders)
+    far_terms = copy(far.at[some], far.at[some], far_sent, far_came, mirror)
+    far_terms_in = copy(far, far, far_sent, far_came, mirror)
+    far_goals_out = copy(far_goals.at[some], far_goals.at[some], far_goal_sent, far_goal_came, mirror)
+    far_goals_in = copy(far_goals, far_goals, far_goal_sent, far_goal_came, mirror)
+
     others = pl.ds(0, team - 1)
     all_goals = copy(goals.at[others], goals.at[others], goal_sent, goal_came, mirror)
     all_terms = [copy(got.at[g, others], got.at[g, others], sent.at[g], came.at[g], mirror) for g in range(strips)]
@@ -267,8 +287,10 @@
     all_final = copy(parts.at[but_own], parts.at[but_own], final_sent, final_came, mirror)
 
     barrier = pltpu.get_barrier_semaphore()
-    for device in [half * team + member(k) for k in range(1, team)] + [mirror, ahead, behind]:
-        pl.semaphore_signal(barrier, inc=1, device_id=at(device), device_id_type=pl.DeviceIdType.MESH)
+    for o in range(1, devices):
+        pl.semaphore_signal(
+            barrier, inc=1, device_id=at(lax.rem(me + o, devices)), device_id_type=pl.DeviceIdType.MESH
+        )
     for t in range(fine_rows // 8):
         p_copy(t).start()
     for transfer in small:
@@ -327,11 +349,13 @@
         return 0
 
     lax.fori_loop(0, fine_rows // 16, prepare, 0)
-    pl.semaphore_wait(barrier, team + 2)
+    pl.semaphore_wait(barrier, devices - 1)
     halo_up.start()
     halo_down.start()
     for k in range(1, team):
         goal_copy(k).start()
+    for h in range(holders):
+        far_goal(h).start()
 
     even = one_if(iota((q, q * KA), 1) // KA == iota((q, q * KA), 0)).astype(jnp.bfloat16)
 
@@ -424,6 +448,8 @@
             rows = whole_rows(chunk, KS * PIECE)
             for pair in range(q):
                 term_ref[pair, rows, :] = stage[pair * SPREAD : pair * SPREAD + KS * PIECE, :].astype(jnp.bfloat16)
+            for h in range(holders):
+                far_part(h, chunk).start()
             for k in range(1, team):
                 term_part(k, chunk).start()
 
@@ -440,35 +466,48 @@
     all_terms[0].wait_recv()
     keep[0].wait()
 
-    def everyone(row, copies):
-        return jnp.concatenate([jnp.broadcast_to(goals[j, row : row + 1, :], (copies, count)) for j in range(team)], axis=1)
-
-    coarse = everyone(0, KA)
-    slot = everyone(1, 2 * KA)
-    slot_hot = one_if(slot == iota(slot.shape, 0).astype(jnp.float32)).astype(jnp.bfloat16)
-
-    def half_sums(which, n):
+    def everyone(rows, row, copies):
+        return jnp.concatenate([jnp.broadcast_to(rows[j, row : row + 1, :], (copies, count)) for j in range(team)], axis=1)
+
+    def hot_slots(rows):
+        slot = everyone(rows, 1, 2 * KA)
+        return one_if(slot == iota(slot.shape, 0).astype(jnp.float32)).astype(jnp.bfloat16)
+
+    coarse, slot_hot = everyone(goals, 0, KA), hot_slots(goals)
+
+    def sums_of(coarse, slot_hot, values, which, n):
         first = (which * team + first_owner(n)) * coarse_rows
         pieces = []
         for j in range(batch * coarse_rows):
             one = one_if(coarse == (first + j).astype(jnp.float32))
             pieces.append(slot_hot * jnp.concatenate([one, one], axis=0).astype(jnp.bfloat16))
-        return jnp.dot(
-            jnp.concatenate(pieces, axis=0), got[lax.div(n, batches)].reshape(-1, LANES), preferred_element_type=jnp.float32
-        )
+        return jnp.dot(jnp.concatenate(pieces, axis=0), values, preferred_element_type=jnp.float32)
+
+    def half_sums(which, n):
+        return sums_of(coarse, slot_hot, got[lax.div(n, batches)].reshape(-1, LANES), which, n)
+
+    def crosses(n):
+        return jnp.logical_not(both_hold) | (n >= batches)
 
     steps = strips * batches
 
+    def prepared(n):
+        sent_sums[n] = half_sums(1 - half, n).astype(jnp.bfloat16)
+
     def cross(n, _):
-        sent_sums[n] = half_sums(1 - half, n).astype(jnp.bfloat16)
-
-        @pl.when(n < FLIGHT)
-        def _():
+        @pl.when(crosses(n))
+        def _():
+            prepared(n)
             cross_copy(n).start()
 
         return 0
 
     lax.fori_loop(0, FLIGHT, cross, 0)
+
+    @pl.when(both_hold)
+    def _():
+        far_goals_in.wait_recv()
+        far_terms_in.wait_recv()
 
     def finish(n, _):
         @pl.when(n == batches - FLIGHT)
@@ -477,19 +516,30 @@
                 all_terms[g].wait_recv()
                 keep[g].wait()
 
-        @pl.when(n < steps - FLIGHT)
-        def _():
-            cross(n + FLIGHT, 0)
-
-        own = half_sums(half, n)
-
-        @pl.when(n < steps - FLIGHT)
+        @pl.when((n < steps - FLIGHT) & crosses(n + FLIGHT))
+        def _():
+            prepared(n + FLIGHT)
+
+        own[...] = half_sums(half, n)
+
+        @pl.when((n < steps - FLIGHT) & crosses(n))
         def _():
             cross_copy(n).wait_send()
+
+        @pl.when((n < steps - FLIGHT) & crosses(n + FLIGHT))
+        def _():
             cross_copy(n + FLIGHT).start()
 
-        cross_copy(n).wait_recv()
-        final[n] = (own + got_sums[n].astype(jnp.float32)).astype(jnp.bfloat16)
+        @pl.when(crosses(n))
+        def _():
+            cross_copy(n).wait_recv()
+            final[n] = (own[...] + got_sums[n].astype(jnp.float32)).astype(jnp.bfloat16)
+
+        @pl.when(jnp.logical_not(crosses(n)))
+        def _():
+            more = sums_of(everyone(far_goals, 0, KA), hot_slots(far_goals), far[...].reshape(-1, LANES), half, n)
+            final[n] = (own[...] + more).astype(jnp.bfloat16)
+
         for b in range(batch):
             owner = first_owner(n) + b
 
@@ -511,6 +561,8 @@
         all_terms[g].wait_send()
     for n in range(steps - FLIGHT, steps):
         cross_copy(n).wait_send()
+    far_terms.wait_send()
+    far_goals_out.wait_send()
     all_final.wait_send()
     all_final.wait_recv()
     for column in range(parts.shape[0]):
@@ -558,6 +610,9 @@
             pltpu.VMEM((strips * coarse_rows, members, LANES), bf16),
             pltpu.VMEM((strips * coarse_rows, members, LANES), bf16),
             pltpu.VMEM((width // LANES, coarse_rows * KC, LANES), bf16),
+            pltpu.VMEM((team, count, LANES), bf16),
+            pltpu.VMEM((team, KA, count), f32),
+            pltpu.VMEM((members, LANES), f32),
             dma((chunks,)),
             dma((fine_rows // 8,)),
             dma((4,)),
@@ -572,6 +627,10 @@
             dma,
             dma,
             dma((strips,)),
+            dma,
+            dma,
+            dma,
+            dma,
         ],
         compiler_params=pltpu.CompilerParams(
             collective_id=0, has_side_effects=True, vmem_limit_bytes=60 * 1024 * 1024

time: 52.4 us -> 50.5 us (0.964)
  Pallas kernels: 50.2 us -> 48.2 us
    pallas_call x1, Pallas kernels: 50.2 us -> 48.2 us  [by_halves(): pl.pallas_call(functools.partial(halves_kernel, pair_count, devices), in_...]
where the time goes in v5:
time: 50.5 us; the launch traced here: 50.3 us
  Pallas kernels  48.2 us (95%)
  other arithmetic  2.08 us (4%)
    pallas_call x1, Pallas kernels, by_halves(): pl.pallas_call(functools.partial(halves_kernel, pair_count, devices), in_...  48.2 us
    convert_element_type x1, other arithmetic, body(): return result.reshape(fine_rows // RATIO, KC, width).astype(jnp.float32)  2.08 us

profile of v5, /device:TPU:0, one launch (start us, length us, event | category | flops | bytes accessed | tf_op | source)
XLA Modules:
  0.0 50.3 jit_solution(3737563754994154684)
XLA Ops:
  0.0 48.2 %shard_map.64 = bf16[64,4096]{1,0:T(8,128)(2,1)} custom-call(bf16[64,256,128]{2,1,0:T(8,128)(2,1)} %bitcast.16, bf16[2048,128]{1,0:T(8,128)(2,1)} %bitcast.18, s32[8,64]{1,0:T(8,128)} %bitcast.19, s32[8,64]{1,0:T(8,128)} %bitcast.20, s32[2,64]{1,0:T(2,128)} %bitcast.21, s32[1,64]{1,0:T(1,128)} %bitcast.22), custom_call_target="tpu_custom_call" | custom-call | tf_op jit(solution)/shard_map/pallas_call | solution.py:586
  48.2 2.1 %convert.1 = f32[4,16,4096]{2,1,0:T(8,128)} convert(bf16[4,16,4096]{2,1,0:T(8,128)(2,1)} %bitcast.17) | non-fusion elementwise | flops 262144 | bytes 1572864 | tf_op jit(solution)/shard_map/convert_element_type | solution.py:676

commit v6 on v5

--- a/solution.py
+++ b/solution.py
@@ -162,7 +162,7 @@
 PIECE = 16
 SPREAD = 40
 AFTER = 2
-FLIGHT = 3
+FLIGHT = 2
 SHARE = 2
 
 
@@ -268,7 +268,7 @@
     def far_part(h, chunk):
         rows = whole_rows(chunk, KS * PIECE)
         to = lax.rem(h * SHARE + mine, team) // SHARE * SHARE
-        place = (to ^ (team // 2 - turn)) * strips
+        place = (to ^ (team // 2 - turn)) * strips + strips - 1
         return copy(term_ref.at[place, rows], far.at[mine, rows], far_sent, far_came, far_team + to)
 
     def far_goal(h):
@@ -448,10 +448,10 @@
             rows = whole_rows(chunk, KS * PIECE)
             for pair in range(q):
                 term_ref[pair, rows, :] = stage[pair * SPREAD : pair * SPREAD + KS * PIECE, :].astype(jnp.bfloat16)
+            for k in range(1, team):
+                term_part(k, chunk).start()
             for h in range(holders):
                 far_part(h, chunk).start()
-            for k in range(1, team):
-                term_part(k, chunk).start()
 
         return 0
 
@@ -486,10 +486,11 @@
     def half_sums(which, n):
         return sums_of(coarse, slot_hot, got[lax.div(n, batches)].reshape(-1, LANES), which, n)
 
+    steps = strips * batches
+
     def crosses(n):
-        return jnp.logical_not(both_hold) | (n >= batches)
-
-    steps = strips * batches
+        return jnp.logical_not(both_hold) | (n < steps - batches)
+
 
     def prepared(n):
         sent_sums[n] = half_sums(1 - half, n).astype(jnp.bfloat16)
@@ -503,11 +504,6 @@
         return 0
 
     lax.fori_loop(0, FLIGHT, cross, 0)
-
-    @pl.when(both_hold)
-    def _():
-        far_goals_in.wait_recv()
-        far_terms_in.wait_recv()
 
     def finish(n, _):
         @pl.when(n == batches - FLIGHT)
@@ -515,6 +511,11 @@
             for g in range(1, strips):
                 all_terms[g].wait_recv()
                 keep[g].wait()
+
+        @pl.when(both_hold & (n == steps - batches))
+        def _():
+            far_goals_in.wait_recv()
+            far_terms_in.wait_recv()
 
         @pl.when((n < steps - FLIGHT) & crosses(n + FLIGHT))
         def _():
@@ -560,7 +561,11 @@
     for g in range(strips):
         all_terms[g].wait_send()
     for n in range(steps - FLIGHT, steps):
-        cross_copy(n).wait_send()
+
+        @pl.when(crosses(n))
+        def _():
+            cross_copy(n).wait_send()
+
     far_terms.wait_send()
     far_goals_out.wait_send()
     all_final.wait_send()

time: 50.5 us -> 49.1 us (0.972)
  Pallas kernels: 48.2 us -> 46.9 us
    pallas_call x1, Pallas kernels: 48.2 us -> 46.9 us  [by_halves(): pl.pallas_call(functools.partial(halves_kernel, pair_count, devices), in_...]
where the time goes in v6:
time: 49.1 us; the launch traced here: 49 us
  Pallas kernels  46.9 us (96%)
  other arithmetic  2.08 us (4%)
    pallas_call x1, Pallas kernels, by_halves(): pl.pallas_call(functools.partial(halves_kernel, pair_count, devices), in_...  46.9 us
    convert_element_type x1, other arithmetic, body(): return result.reshape(fine_rows // RATIO, KC, width).astype(jnp.float32)  2.08 us

profile of v6, /device:TPU:0, one launch (start us, length us, event | category | flops | bytes accessed | tf_op | source)
XLA Modules:
  0.0 49.0 jit_solution(11853457224918123335)
XLA Ops:
  0.0 46.9 %shard_map.64 = bf16[64,4096]{1,0:T(8,128)(2,1)} custom-call(bf16[64,256,128]{2,1,0:T(8,128)(2,1)} %bitcast.16, bf16[2048,128]{1,0:T(8,128)(2,1)} %bitcast.18, s32[8,64]{1,0:T(8,128)} %bitcast.19, s32[8,64]{1,0:T(8,128)} %bitcast.20, s32[2,64]{1,0:T(2,128)} %bitcast.21, s32[1,64]{1,0:T(1,128)} %bitcast.22), custom_call_target="tpu_custom_call" | custom-call | tf_op jit(solution)/shard_map/pallas_call | solution.py:591
  46.9 2.1 %convert.1 = f32[4,16,4096]{2,1,0:T(8,128)} convert(bf16[4,16,4096]{2,1,0:T(8,128)(2,1)} %bitcast.17) | non-fusion elementwise | flops 262144 | bytes 1572864 | tf_op jit(solution)/shard_map/convert_element_type | solution.py:681

commit v7 on v6

--- a/solution.py
+++ b/solution.py
@@ -172,8 +172,8 @@
 
 def halves_kernel(
     pair_count, devices,
-    a_hbm, p_hbm, cols_hbm, group_hbm, slots_hbm, aggregate_hbm, out_ref,
-    a_ref, p_ref, cols_ref, groups_ref, slots_ref, agg_ref,
+    a_hbm, p_hbm, small_hbm, out_ref,
+    a_ref, p_ref, small_ref,
     tiles, diag, turned, code, pick, stage, products, sums, term_ref, got, goals, sent_sums, got_sums, final, parts, far, far_goals, own,
     a_came, p_came, small_came, halo_sent, halo_came, sent, came, goal_sent, goal_came, cross_sent, cross_came, final_sent, final_came, self_came, far_sent, far_came, far_goal_sent, far_goal_came,
 ):
@@ -215,12 +215,7 @@
         rows = whole_rows(t, 8 * q)
         return pltpu.make_async_copy(p_hbm.at[rows], p_ref.at[rows], p_came.at[t])
 
-    small = [
-        pltpu.make_async_copy(src, dst, small_came.at[i])
-        for i, (src, dst) in enumerate(
-            [(cols_hbm, cols_ref), (group_hbm, groups_ref), (slots_hbm, slots_ref), (aggregate_hbm, agg_ref)]
-        )
-    ]
+    small = pltpu.make_async_copy(small_hbm, small_ref, small_came)
     edge = HB * LANES
     inner = fine_rows * LANES
     halo_up = copy(diag.at[pl.ds(inner, edge)], diag.at[pl.ds(0, edge)], halo_sent.at[0], halo_came.at[0], ahead)
@@ -293,8 +288,7 @@
         )
     for t in range(fine_rows // 8):
         p_copy(t).start()
-    for transfer in small:
-        transfer.start()
+    small.start()
     for order in range(chunks):
         a_copy(order).start()
 
@@ -303,14 +297,13 @@
     perm = one_if((r128 // BLK == k128 // BLK) & (k128 % BLK == 2 * (r128 % q) + (r128 % BLK) // q)).astype(jnp.bfloat16)
     low = iota((q, LANES), 1) < BLK
 
-    for transfer in small:
-        transfer.wait()
-    offset = cols_ref[...] - (me * fine_rows + iota((KA, fine_rows), 1)) + HB
+    small.wait()
+    offset = small_ref[:KA, :] - (me * fine_rows + iota((KA, fine_rows), 1)) + HB
     for i in range(fine_rows):
         code[i] = jnp.broadcast_to(offset[:, i : i + 1], (KA, LANES))
     repeat = one_if(iota((KA, q * KA), 1) % KA == iota((KA, q * KA), 0)).astype(jnp.bfloat16)
     pick[...] = lax.dot_general(
-        groups_ref[...].astype(jnp.float32).astype(jnp.bfloat16),
+        small_ref[KA : 2 * KA, :].astype(jnp.float32).astype(jnp.bfloat16),
         repeat,
         (((0,), (0,)), ((), ())),
         preferred_element_type=jnp.float32,
@@ -322,8 +315,8 @@
         place = one_if(term == (fine // PIECE) * (KS * PIECE) + s * PIECE + fine % PIECE).astype(jnp.bfloat16)
         values = jnp.where(
             iota((KA, fine_rows), 0) == 0,
-            jnp.broadcast_to(agg_ref[...], (KA, fine_rows)),
-            jnp.broadcast_to(slots_ref[s : s + 1, :], (KA, fine_rows)),
+            jnp.broadcast_to(small_ref[2 * KA + KS : 2 * KA + KS + 1, :], (KA, fine_rows)),
+            jnp.broadcast_to(small_ref[2 * KA + s : 2 * KA + s + 1, :], (KA, fine_rows)),
         )
         values = values.astype(jnp.float32).astype(jnp.bfloat16)
         goal_rows.append(jnp.dot(values, place, preferred_element_type=jnp.float32))
@@ -448,7 +441,7 @@
             rows = whole_rows(chunk, KS * PIECE)
             for pair in range(q):
                 term_ref[pair, rows, :] = stage[pair * SPREAD : pair * SPREAD + KS * PIECE, :].astype(jnp.bfloat16)
-            for k in range(1, team):
+            for k in range(team - 1, 0, -1):
                 term_part(k, chunk).start()
             for h in range(holders):
                 far_part(h, chunk).start()
@@ -457,7 +450,7 @@
 
     lax.fori_loop(0, groups + AFTER, step, 0)
     for g in range(1, strips):
-        for k in range(1, team):
+        for k in range(team - 1, 0, -1):
             term_rest(k, g).start()
     keep = [pltpu.make_async_copy(term_ref.at[strip(mine, g)], got.at[g, mine], self_came.at[g]) for g in range(strips)]
     for transfer in keep:
@@ -586,20 +579,18 @@
     members = team * KC
     a = a_tiles.reshape(fine_rows, KA, q, LANES).transpose(0, 2, 1, 3).reshape(fine_rows, q * KA, LANES)
     p = p_tiles.reshape(fine_rows // 8, 8, q, LANES).transpose(0, 2, 1, 3).reshape(fine_rows * q, LANES)
+    small = jnp.concatenate([a_cols.T, tile_group.T, coarse_slots.T, aggregate.reshape(1, fine_rows)], axis=0)
     bf16, f32, i32 = jnp.bfloat16, jnp.float32, jnp.int32
     dma = pltpu.SemaphoreType.DMA
     return pl.pallas_call(
         functools.partial(halves_kernel, pair_count, devices),
-        in_specs=[pl.BlockSpec(memory_space=pltpu.HBM)] * 6,
+        in_specs=[pl.BlockSpec(memory_space=pltpu.HBM)] * 3,
         out_specs=pl.BlockSpec(memory_space=pltpu.VMEM),
         out_shape=jax.ShapeDtypeStruct((coarse_rows * KC, width), bf16),
         scratch_shapes=[
             pltpu.VMEM(a.shape, bf16),
             pltpu.VMEM(p.shape, bf16),
-            pltpu.VMEM((KA, fine_rows), i32),
-            pltpu.VMEM((KA, fine_rows), i32),
-            pltpu.VMEM((KS, fine_rows), i32),
-            pltpu.VMEM((1, fine_rows), i32),
+            pltpu.VMEM((2 * KA + KS + 1, fine_rows), i32),
             pltpu.VMEM((16 * q, LANES), f32),
             pltpu.VMEM(((fine_rows + 2 * HB) * LANES, LANES), bf16),
             pltpu.VMEM((fine_rows * BLK, BLK), bf16),
@@ -620,7 +611,7 @@
             pltpu.VMEM((members, LANES), f32),
             dma((chunks,)),
             dma((fine_rows // 8,)),
-            dma((4,)),
+            dma,
             dma((2,)),
             dma((2,)),
             dma((strips,)),
@@ -638,9 +629,9 @@
             dma,
         ],
         compiler_params=pltpu.CompilerParams(
-            collective_id=0, has_side_effects=True, vmem_limit_bytes=60 * 1024 * 1024
+            collective_id=0, has_side_effects=True, vmem_limit_bytes=53 * 1024 * 1024
         ),
-    )(a, p, a_cols.T, tile_group.T, coarse_slots.T, aggregate.reshape(1, fine_rows))
+    )(a, p, small)
 
 
 def routed(terms, coarse_slots, aggregate):

time: 49.1 us -> 46.4 us (0.945)
  Pallas kernels: 46.9 us -> 44.4 us
    pallas_call x1, Pallas kernels: 46.9 us -> 44.4 us  [by_halves(): pl.pallas_call(functools.partial(halves_kernel, pair_count, devices), in_...]
    convert_element_type x1, other arithmetic: 2.08 us -> 1.04 us  [body(): return result.reshape(fine_rows // RATIO, KC, width).astype(jnp.float32)]
    concatenate x0 -> x1, other arithmetic: none -> 0.74 us  [by_halves(): jnp.concatenate([a_cols.T, tile_group.T, coarse_slots.T, aggregate.reshap...]
where the time goes in v7:
time: 46.4 us; the launch traced here: 46.2 us
  Pallas kernels  44.4 us (96%)
  other arithmetic  1.78 us (4%)
    pallas_call x1, Pallas kernels, by_halves(): pl.pallas_call(functools.partial(halves_kernel, pair_count, devices), in_...  44.4 us
    convert_element_type x1, other arithmetic, body(): return result.reshape(fine_rows // RATIO, KC, width).astype(jnp.float32)  1.04 us

profile of v7, /device:TPU:0, one launch (start us, length us, event | category | flops | bytes accessed | tf_op | source)
XLA Modules:
  0.0 46.2 jit_solution(18234165771671923540)
XLA Ops:
  0.0 0.7 %pad_add_fusion.small_hbm = s32[19,64]{1,0:T(8,128)S(1)} fusion(s32[1,64]{1,0:T(1,128)} %bitcast.22, s32[2,64]{1,0:T(2,128)} %bitcast.21, s32[8,64]{1,0:T(8,128)} %bitcast.19, s32[8,64]{1,0:T(8,128)} %bitcast.20), kind=kLoop, calls=%fused_computation | loop fusion | flops 3648 | bytes 9728 | tf_op jit(solution)/shard_map/concatenate | solution.py:582
  0.7 44.4 %shard_map.64 = bf16[64,4096]{1,0:T(8,128)(2,1)S(1)} custom-call(bf16[64,256,128]{2,1,0:T(8,128)(2,1)} %bitcast.17, bf16[2048,128]{1,0:T(8,128)(2,1)} %bitcast.18, s32[19,64]{1,0:T(8,128)S(1)} %pad_add_fusion.small_hbm), custom_call_target="tpu_custom_call" | custom-call | tf_op jit(solution)/shard_map/pallas_call | solution.py:585
  45.2 1.0 %convert.1 = f32[4,16,4096]{2,1,0:T(8,128)} convert(bf16[4,16,4096]{2,1,0:T(8,128)(2,1)S(1)} %bitcast.16) | non-fusion elementwise | flops 262144 | bytes 1572864 | tf_op jit(solution)/shard_map/convert_element_type | solution.py:672
